TPU v7x, 128 devices: a whole 4x4x4 slice. The times are simulated.
128 devices in a mesh: row: 8 (over y, core), col: 8 (over z, x_lo), ch: 2 (over x_hi).
Axes of the slice: x: 4 (x_hi: 2, x_lo: 2; x = x_hi * 2 + x_lo), y: 4, z: 4, core: 2. Of those that a mesh axis runs over, the one named last changes fastest.
Arguments:
- pair: bfloat16 [896, 896, 128], P('row', 'col'), may hold values from -6 to 6
- pair_mask: int32 [896, 896], P('row', 'col'), may hold values 0 or 1
- ln_in_gain: float32 [128], replicated, may hold values from 0.1 to 1.9
- w_left_gate: bfloat16 [128, 128], P(None, 'ch'), may hold values from -0.5 to 0.5
- w_left_proj: bfloat16 [128, 128], P(None, 'ch'), may hold values from -0.5 to 0.5
- w_right_gate: bfloat16 [128, 128], P(None, 'ch'), may hold values from -0.5 to 0.5
- w_right_proj: bfloat16 [128, 128], P(None, 'ch'), may hold values from -0.5 to 0.5
- w_gate: bfloat16 [128, 128], replicated, may hold values from -0.5 to 0.5
- ln_out_gain: float32 [128], replicated, may hold values from 0.1 to 1.9
- w_out: bfloat16 [128, 128], replicated, may hold values from -0.5 to 0.5
Outputs:
- update: bfloat16 [896, 896, 128], P('row', ('col', 'ch'))
All inputs are finite; a program needn't handle non-finite values. No bound on the sum of `pair_mask` on one device may be relied on, other than what follows from the above.
Results may differ from a plain program's by a relative error of at most 0.025.
Values may be sent and summed in bfloat16 or wider, within the bound.
No kernel may reach another device: no remote copies, remote signals or barrier semaphores. Data moves between devices by JAX's collectives and lax.ppermute only.
A program may use at most 192 MiB of HBM per device.

v0:
```python
import jax
import jax.numpy as jnp
from jax import lax
from jax.sharding import PartitionSpec as P

epsilon = 1e-05


def normalize(values, gain_vec):
    center_val = jnp.mean(values, axis=-1, keepdims=True)
    centered = values - center_val
    spread = jnp.mean(centered * centered, axis=-1, keepdims=True)
    return centered * lax.rsqrt(spread + epsilon) * gain_vec


def shards(
    pair,
    pair_mask,
    ln_in_gain,
    w_left_gate,
    w_left_proj,
    w_right_gate,
    w_right_proj,
    w_gate,
    ln_out_gain,
    w_out,
):
    tile_size = pair.shape[0]
    hidden_part = w_left_gate.shape[1]
    ch_count = lax.axis_size("ch")
    half_cols = tile_size // ch_count
    pair_normed = normalize(pair.astype(jnp.float32), ln_in_gain).astype(jnp.bfloat16)
    valid_pairs = pair_mask.astype(jnp.float32)[:, :, None]

    def project(source, weight):
        return jnp.dot(source, weight, preferred_element_type=jnp.float32)

    left_vals = (
        valid_pairs
        * jax.nn.sigmoid(project(pair_normed, w_left_gate))
        * project(pair_normed, w_left_proj)
    ).astype(jnp.bfloat16)
    right_vals = (
        valid_pairs
        * jax.nn.sigmoid(project(pair_normed, w_right_gate))
        * project(pair_normed, w_right_proj)
    ).astype(jnp.bfloat16)
    left_flat = left_vals.reshape(tile_size, tile_size * hidden_part)
    gathered = lax.all_gather(left_flat, "col", axis=1, tiled=True)
    left_block = gathered
    left_block = left_block.reshape(tile_size, lax.axis_size("row") * tile_size, hidden_part)
    product = jnp.einsum("kic,kjc->ijc", left_block, right_vals, preferred_element_type=jnp.float32)
    summed = lax.psum_scatter(
        product.reshape(lax.axis_size("row") * tile_size, tile_size * hidden_part).astype(
            jnp.bfloat16
        ),
        "row",
        scatter_dimension=0,
        tiled=True,
    ).astype(jnp.float32)
    hidden = summed.reshape(tile_size, tile_size, hidden_part)
    ch_index = lax.axis_index("ch")
    pair_half = lax.dynamic_slice_in_dim(pair_normed, ch_index * half_cols, half_cols, 1)
    gate_vals = jax.nn.sigmoid(project(pair_half, w_gate))
    channels = hidden_part * ch_count
    center_val = (
        lax.psum(jnp.sum(hidden, axis=-1).astype(jnp.bfloat16), "ch").astype(jnp.float32) / channels
    )
    centered = hidden - center_val[:, :, None]
    spread = (
        lax.psum(jnp.sum(centered * centered, axis=-1).astype(jnp.bfloat16), "ch").astype(
            jnp.float32
        )
        / channels
    )
    gain_part = lax.dynamic_slice_in_dim(ln_out_gain, ch_index * hidden_part, hidden_part, 0)
    hidden_normed = (centered * lax.rsqrt(spread + epsilon)[:, :, None] * gain_part).astype(
        jnp.bfloat16
    )
    weight_part = lax.dynamic_slice_in_dim(w_out, ch_index * hidden_part, hidden_part, 0)
    partial_out = project(hidden_normed, weight_part)
    projected = lax.psum_scatter(
        partial_out.astype(jnp.bfloat16), "ch", scatter_dimension=1, tiled=True
    ).astype(jnp.float32)
    return (gate_vals * projected).astype(jnp.bfloat16)


def solution(mesh):
    in_specs = (
        P("row", "col", None),
        P("row", "col"),
        P(),
        P(None, "ch"),
        P(None, "ch"),
        P(None, "ch"),
        P(None, "ch"),
        P(),
        P(),
        P(),
    )
    out_specs = P("row", ("col", "ch"), None)
    return jax.shard_map(shards, mesh=mesh, in_specs=in_specs, out_specs=out_specs, check_vma=False)
```

profile of v0, /device:TPU:1, one launch (start us, length us, event | category | flops | bytes accessed | tf_op | source)
XLA Modules:
  0.0 542.5 jit_solution(11719199353094883291)
XLA Ops:
  6.5 0.0 copy-start
  6.5 0.0 all-gather.2.cloned.1.call-start
  6.6 3.1 convert_reduce_fusion
  9.7 0.0 copy-done.1
  9.7 4.2 fusion.6
  14.0 0.0 copy-done.5
  14.0 0.0 copy-done.8
  14.0 0.0 copy-start.6
  14.0 4.1 fusion.8
  18.1 0.0 copy-done.6
  18.1 0.0 copy-start.2
  18.1 0.0 copy-start.10
  18.1 2.2 fusion.14
  20.4 3.5 multiply_convert_fusion.1
  23.9 4.5 copy.26
  28.4 0.0 all-gather.2.cloned.1.call-update
  28.4 0.0 copy-start.11
  28.4 0.0 reduce-scatter.7.cloned.1.call-start
  28.5 2.2 fusion.17
  30.7 3.5 multiply_convert_fusion.2
  34.2 283.9 %all-gather.2.cloned.1.call-done = bf16[112,57344]{0,1:T(8,128)(2,1)} async-done(((bf16[112,7168]{0,1:T(8,128)(2,1)}), bf16[112,57344]{0,1:T(8,128)(2,1)}) %all-gather.2.cloned.1.call-update) | async-done | bytes 12845072 | tf_op jit(solution)/shard_map/all_gather | solution.py:49
  318.0 24.4 %convert_bitcast_fusion = bf16[896,112,64]{0,1,2:T(8,128)(2,1)} fusion(bf16[112,896,64]{0,2,1:T(8,128)(2,1)} %bitcast.40, bf16[112,112,64]{1,2,0:T(8,128)(2,1)} %multiply_convert_fusion.2), kind=kOutput, calls=%fused_computation.2 | convolution fusion | flops 1445068800 | bytes 27295744 | tf_op jit(solution)/shard_map/kic,kjc->ijc/dot_general | solution.py:52
  342.4 14.1 %copy.29 = bf16[896,112,64]{0,2,1:T(8,128)(2,1)} copy(bf16[896,112,64]{0,1,2:T(8,128)(2,1)} %convert_bitcast_fusion) | data formatting | bytes 25690112 | tf_op jit(solution)/shard_map/convert_element_type | solution.py:54
  356.5 17.5 %copy.35 = bf16[896,7168]{1,0:T(8,128)(2,1)} copy(bf16[896,7168]{0,1:T(8,128)(2,1)} %bitcast.39) | data formatting | bytes 25690112
  373.9 0.0 reduce-scatter.7.cloned.1.call-update
  374.0 0.0 reduce-scatter.9.cloned.1.call-start
  374.0 0.6 copy-done.12
  374.6 0.1 dynamic_slice.10
  374.7 73.6 %reduce-scatter.7.cloned.1.call-done = bf16[112,7168]{1,0:T(8,128)(2,1)} async-done(((bf16[896,7168]{1,0:T(8,128)(2,1)}), bf16[112,7168]{1,0:T(8,128)(2,1)}) %reduce-scatter.7.cloned.1.call-update) | async-done | bytes 1605648
  448.3 3.2 copy.36
  451.5 0.7 reduce
  452.2 0.1 copy.30
  452.3 9.5 %psum.14 = bf16[112,112]{1,0:T(8,128)(2,1)S(1)} all-reduce(bf16[112,112]{1,0:T(8,128)(2,1)S(1)} %copy.30), channel_id=1, replica_groups=mesh['row'=8,'col'=8,'ch'=2] {'ch'}, use_global_device_ids=true, to_apply=%region_4.0 | all-reduce | flops 12544 | bytes 50176 | tf_op jit(solution)/shard_map/psum | solution.py:67
  461.9 0.1 copy.31
  462.0 0.9 multiply_reduce_fusion
  462.9 0.1 copy.32
  463.0 6.9 %psum.15 = bf16[112,112]{1,0:T(8,128)(2,1)S(1)} all-reduce(bf16[112,112]{1,0:T(8,128)(2,1)S(1)} %copy.32), channel_id=1, replica_groups=mesh['row'=8,'col'=8,'ch'=2] {'ch'}, use_global_device_ids=true, to_apply=%region_6.0 | all-reduce | flops 12544 | bytes 50176 | tf_op jit(solution)/shard_map/psum | solution.py:71
  469.9 0.1 copy.33
  470.0 2.0 multiply_convert_fusion
  472.0 3.6 copy.34
  475.6 0.0 copy-done
  475.6 1.1 convolution_convert_fusion
  476.7 0.8 copy.37
  477.5 2.5 copy.49
  480.0 0.0 reduce-scatter.9.cloned.1.call-update
  480.0 52.0 %reduce-scatter.9.cloned.1.call-done = bf16[56,14336]{1,0:T(8,128)(2,1)} async-done(((bf16[112,14336]{1,0:T(8,128)(2,1)}), bf16[56,14336]{1,0:T(8,128)(2,1)}) %reduce-scatter.9.cloned.1.call-update) | async-done | bytes 1605648
  532.1 1.6 copy.40
  533.7 2.2 multiply_convert_fusion.3
  (20 shorter events, 0.1 us)
Async XLA Ops:
  6.5 469.1 %copy-start = (bf16[128,128]{1,0:T(8,128)(2,1)S(1)}, bf16[128,128]{1,0:T(8,128)(2,1)}, u32[]{:S(2)}) copy-start(bf16[128,128]{1,0:T(8,128)(2,1)} %param.19) | copy-start | bytes 98308
  6.5 3.2 copy-start.1
  6.5 7.4 %copy-start.5 = (s32[112,112]{1,0:T(8,128)S(1)}, s32[112,112]{1,0:T(8,128)}, u32[]{:S(2)}) copy-start(s32[112,112]{1,0:T(8,128)} %param.11) | copy-start | bytes 150532
  6.5 7.5 %copy-start.8 = (f32[128]{0:T(128)S(1)}, f32[128]{0:T(128)}, u32[]{:S(2)}) copy-start(f32[128]{0:T(128)} %param.12) | copy-start | bytes 1540
  6.5 311.5 %all-gather.2.cloned.1.call-start = ((), (), s32[]{:S(2)}) async-start(), calls=%async_computation.2 | async-start | bytes 16515072 | tf_op jit(solution)/shard_map/all_gather | solution.py:49
  14.0 4.1 copy-start.6
  18.1 2.2 copy-start.2
  18.1 2.2 copy-start.10
  23.9 4.6 copy-start.3
  23.9 4.6 copy-start.7
  28.4 2.3 copy-start.11
  28.4 419.9 %reduce-scatter.7.cloned.1.call-start = ((), (), s32[]{:S(2)}) async-start(), calls=%async_computation.3 | async-start | bytes 14450688
  373.9 0.7 copy-start.12
  374.0 158.1 %reduce-scatter.9.cloned.1.call-start = ((), (), s32[]{:S(2)}) async-start(), calls=%async_computation.4 | async-start | bytes 4816896
  480.0 53.7 %copy-start.4 = (bf16[112,112,128]{2,1,0:T(8,128)(2,1)S(1)}, bf16[112,112,128]{2,1,0:T(8,128)(2,1)}, u32[]{:S(2)}) copy-start(bf16[112,112,128]{2,1,0:T(8,128)(2,1)} %copy-done.2) | copy-start | bytes 9633796
  480.0 53.7 %copy-start.9 = (bf16[128,128]{1,0:T(8,128)(2,1)S(1)}, bf16[128,128]{1,0:T(8,128)(2,1)}, u32[]{:S(2)}) copy-start(bf16[128,128]{1,0:T(8,128)(2,1)} %param.17) | copy-start | bytes 98308
Sparse Core Ops, SparseCore 0:
  28.5 289.4 all-gather.1
  374.1 74.1 reduce-scatter.6
  480.2 51.8 reduce-scatter.8
where the time goes:
time: 543 us; the launch traced here: 542 us
  waiting for transfers between devices  410 us (76%)
  local copies, waits for them, and re-layouts  49 us (9%)
  matrix products  39 us (7%)
  blocking collectives  16.4 us (3%)
  other arithmetic  15.1 us (3%)
  between operations  13.4 us (2%)
    all_gather x1, waiting for transfers between devices, shards(): gathered = lax.all_gather(left_flat, 'col', axis=1, tiled=True)  284 us
    unnamed x5, waiting for transfers between devices  126 us
    unnamed x31, local copies, waits for them, and re-layouts  26.3 us
    dot_general x1, matrix products, shards(): jnp.einsum('kic,kjc->ijc', left_block, right_vals, preferred_element_type...  24.4 us
    dot_general x6, matrix products, project(): return jnp.dot(source, weight, preferred_element_type=jnp.float32)  14.7 us
    convert_element_type x1, local copies, waits for them, and re-layouts, shards(): product.reshape(lax.axis_size('row') * tile_size, tile_size * hidden_part)  14.1 us
  transfers between devices with their start and end apart: 3, of which 3 were waited for; matrix products, arithmetic and copies ran while one was open for 1% of the time, Pallas kernels for 0%

commit v1 on v0

v1 whole, which is shorter than its diff:
```python
import jax
import jax.numpy as jnp
from jax import lax
from jax.experimental import pallas as pl
from jax.experimental.pallas import tpu as pltpu
from jax.sharding import PartitionSpec as P

epsilon = 1e-05
f32 = jnp.float32
bf16 = jnp.bfloat16
lanes = 128
chunk = 16


def sigmoid(values):
    return 0.5 * jnp.tanh(0.5 * values) + 0.5


def project_kernel(
    pair_ref,
    mask_ref,
    gain_ref,
    left_gate_ref,
    left_proj_ref,
    right_gate_ref,
    right_proj_ref,
    gate_weight_ref,
    message_ref,
    gate_ref,
    weight_scr,
    normed_scr,
    mask_scr,
    turn_scr,
):
    tile = pair_ref.shape[1]
    part = left_gate_ref.shape[1]
    half = tile // 2

    @pl.when(pl.program_id(0) == 0)
    def _():
        joined = jnp.concatenate(
            [left_gate_ref[...], left_proj_ref[...], right_gate_ref[...], right_proj_ref[...]],
            axis=1,
        )
        weight_scr[...] = joined.astype(f32).T.astype(bf16)
        normed_scr[...] = jnp.zeros_like(normed_scr)
        mask_scr[...] = jnp.zeros_like(mask_scr)

    values = pair_ref[...].astype(f32)
    centered = values - jnp.mean(values, axis=-1, keepdims=True)
    spread = jnp.mean(centered * centered, axis=-1, keepdims=True)
    normed = centered * lax.rsqrt(spread + epsilon) * gain_ref[...][None]
    normed_scr[:, :tile, :] = normed.astype(bf16)
    mask_scr[:, :tile] = mask_ref[...].astype(f32)

    own = jnp.where(lax.axis_index("ch") == 0, normed[:, :half], normed[:, half:])
    own = own.reshape(chunk * half, lanes).astype(bf16)
    gate = sigmoid(jnp.dot(own, gate_weight_ref[...], preferred_element_type=f32))
    gate_ref[...] = gate.reshape(gate_ref.shape)

    for k in range(0, chunk, 2):
        source = normed_scr[k : k + 2].reshape(2 * lanes, lanes)
        products = lax.dot_general(
            weight_scr[...], source, (((1,), (1,)), ((), ())), preferred_element_type=f32
        )
        for kk in range(2):
            own_lanes = products[:, kk * lanes : (kk + 1) * lanes]
            valid = mask_scr[k + kk : k + kk + 1, :]
            for side in range(2):
                base = 2 * part * side
                vals = (
                    valid
                    * sigmoid(own_lanes[base : base + part])
                    * own_lanes[base + part : base + 2 * part]
                )
                turn_scr[side, pl.ds(k + kk, part, stride=chunk), :] = vals
    for side in range(2):
        message_ref[:, side] = turn_scr[side].reshape(part, chunk, lanes).astype(bf16)


def product_kernel(left_ref, right_ref, out_ref, right_scr):
    rows, cols = right_ref.shape[0], right_ref.shape[1]
    tile = right_ref.shape[3]
    depth = rows * tile

    @pl.when(pl.program_id(0) == 0)
    def _():
        for q in range(cols):
            block = right_ref[:, q, 0].reshape(depth, lanes)
            right_scr[q * tile : (q + 1) * tile, :] = block.astype(f32).T[:tile].astype(bf16)

    sides = [left_ref[:, p, 0].reshape(depth, lanes) for p in range(left_ref.shape[1])]
    hidden = jnp.dot(
        right_scr[...], jnp.concatenate(sides, axis=1), preferred_element_type=f32
    ).astype(bf16)
    for p in range(left_ref.shape[1]):
        out_ref[p] = hidden[:, p * lanes : (p + 1) * lanes]


def finish_kernel(hidden_ref, gate_ref, gain_ref, weight_ref, out_ref, weight_scr, turn_scr, out_scr):
    channels = hidden_ref.shape[0]
    tile = out_ref.shape[0]

    @pl.when(pl.program_id(0) == 0)
    def _():
        spread_gain = jnp.broadcast_to(gain_ref[...], (channels, channels)).T
        scaled = spread_gain * weight_ref[...].astype(f32)
        part = channels // 2
        for side in range(2):
            turn_scr[pl.ds(side, part, stride=2), :] = scaled[side * part : (side + 1) * part]
        weight_scr[...] = turn_scr[:channels, :].astype(bf16)

    hidden = hidden_ref[:, 0].astype(f32)
    centered = hidden - jnp.mean(hidden, axis=0, keepdims=True)
    spread = jnp.mean(centered * centered, axis=0, keepdims=True)
    normed = centered * lax.rsqrt(spread + epsilon)
    turn_scr[...] = normed.reshape(channels * 8, lanes)
    for j in range(8):
        row = turn_scr[pl.ds(j, channels, stride=8), :].astype(bf16)
        projected = lax.dot_general(
            row, weight_scr[...], (((0,), (0,)), ((), ())), preferred_element_type=f32
        )
        out_scr[pl.ds(j, tile, stride=8), :] = projected[:tile]
    out_ref[:, 0] = (out_scr[...].reshape(tile, 8, lanes) * gate_ref[:, 0]).astype(bf16)


def shards(
    pair,
    pair_mask,
    ln_in_gain,
    w_left_gate,
    w_left_proj,
    w_right_gate,
    w_right_proj,
    w_gate,
    ln_out_gain,
    w_out,
):
    tile, channels = pair.shape[0], pair.shape[2]
    part = w_left_gate.shape[1]
    rows, cols, ch = lax.axis_size("row"), lax.axis_size("col"), lax.axis_size("ch")
    half = tile // ch
    groups = half // 8
    whole = lambda shape: pl.BlockSpec(shape, lambda s: (0,) * len(shape))

    message, gate = pl.pallas_call(
        project_kernel,
        grid=(tile // chunk,),
        in_specs=[
            pl.BlockSpec((chunk, tile, channels), lambda s: (s, 0, 0)),
            pl.BlockSpec((chunk, tile), lambda s: (s, 0)),
            whole((1, channels)),
            whole((channels, part)),
            whole((channels, part)),
            whole((channels, part)),
            whole((channels, part)),
            whole((channels, channels)),
        ],
        out_specs=[
            pl.BlockSpec((part, 2, chunk, lanes), lambda s: (0, 0, s, 0)),
            pl.BlockSpec((chunk, groups, 8, lanes), lambda s: (s, 0, 0, 0)),
        ],
        out_shape=[
            jax.ShapeDtypeStruct((part, 2, tile, lanes), bf16),
            jax.ShapeDtypeStruct((tile, groups, 8, lanes), f32),
        ],
        scratch_shapes=[
            pltpu.VMEM((4 * part, channels), bf16),
            pltpu.VMEM((chunk, lanes, channels), bf16),
            pltpu.VMEM((chunk, lanes), f32),
            pltpu.VMEM((2, part * chunk, lanes), f32),
        ],
        compiler_params=pltpu.CompilerParams(vmem_limit_bytes=24 * 2**20),
        name="project",
    )(
        pair,
        pair_mask,
        ln_in_gain.reshape(1, channels),
        w_left_gate,
        w_left_proj,
        w_right_gate,
        w_right_proj,
        w_gate,
    )

    received = lax.all_to_all(message, ("row", "col"), 0, 0, tiled=True)
    received = received.reshape(rows, cols, 2, tile, lanes)

    pairs = 2
    hidden = pl.pallas_call(
        product_kernel,
        grid=(rows // pairs,),
        in_specs=[
            pl.BlockSpec((rows, pairs, 1, tile, lanes), lambda s: (0, s, 0, 0, 0)),
            pl.BlockSpec((rows, cols, 1, tile, lanes), lambda s: (0, 0, 1, 0, 0)),
        ],
        out_specs=pl.BlockSpec((pairs, cols * tile, lanes), lambda s: (s, 0, 0)),
        out_shape=jax.ShapeDtypeStruct((rows, cols * tile, lanes), bf16),
        scratch_shapes=[pltpu.VMEM((cols * tile, rows * tile), bf16)],
        compiler_params=pltpu.CompilerParams(vmem_limit_bytes=24 * 2**20),
        name="product",
    )(received, received)

    parts = lax.all_to_all(
        hidden.reshape(rows * cols * ch, half, lanes), ("row", "col", "ch"), 0, 0, tiled=True
    )
    parts = parts.reshape(channels, groups, 8, lanes)

    update = pl.pallas_call(
        finish_kernel,
        grid=(groups,),
        in_specs=[
            pl.BlockSpec((channels, 1, 8, lanes), lambda s: (0, s, 0, 0)),
            pl.BlockSpec((tile, 1, 8, lanes), lambda s: (0, s, 0, 0)),
            whole((1, channels)),
            whole((channels, channels)),
        ],
        out_specs=pl.BlockSpec((tile, 1, 8, lanes), lambda s: (0, s, 0, 0)),
        out_shape=jax.ShapeDtypeStruct((tile, groups, 8, lanes), bf16),
        scratch_shapes=[
            pltpu.VMEM((channels, channels), bf16),
            pltpu.VMEM((channels * 8, lanes), f32),
            pltpu.VMEM((tile * 8, lanes), f32),
        ],
        compiler_params=pltpu.CompilerParams(vmem_limit_bytes=24 * 2**20),
        name="finish",
    )(parts, gate, ln_out_gain.reshape(1, channels), w_out)
    return update.reshape(tile, half, channels)


def solution(mesh):
    in_specs = (
        P("row", "col", None),
        P("row", "col"),
        P(),
        P(None, "ch"),
        P(None, "ch"),
        P(None, "ch"),
        P(None, "ch"),
        P(),
        P(),
        P(),
    )
    out_specs = P("row", ("col", "ch"), None)
    return jax.shard_map(shards, mesh=mesh, in_specs=in_specs, out_specs=out_specs, check_vma=False)
```

time: 543 us -> 116 us (0.21)
  waiting for transfers between devices: 410 us -> 0 us
  blocking collectives: 16.4 us -> 89.6 us
  local copies, waits for them, and re-layouts: 49 us -> 7.48 us
  matrix products: 39 us -> 0 us
  Pallas kernels: 0 us -> 18 us
  other arithmetic: 15.1 us -> 0 us
  between operations: 13.4 us -> 0.05 us
    all_gather x1 -> x0, waiting for transfers between devices: 284 us -> none  [shards(): gathered = lax.all_gather(left_flat, 'col', axis=1, tiled=True)]
    unnamed x5 -> x0, waiting for transfers between devices: 126 us -> none
    all_to_all x0 -> x2, blocking collectives: none -> 89.6 us  [the longest x1 56.8 us: shards(): received = lax.all_to_all(message, ('row', 'col'), 0, 0, tiled=True)]
    dot_general x7 -> x0, matrix products: 39 us -> none  [the longest x1 24.4 us: shards(): jnp.einsum('kic,kjc->ijc', left_block, right_vals, preferred_element_type...]
    convert_element_type x3 -> x0, local copies, waits for them, and re-layouts: 22.2 us -> none  [the longest x1 14.1 us: shards(): product.reshape(lax.axis_size('row') * tile_size, tile_size * hidden_part)]
    unnamed x31 -> x16, local copies, waits for them, and re-layouts: 26.3 us -> 7.48 us
    pallas_call x0 -> x3, Pallas kernels: none -> 18 us  [the longest x1 8.74 us: shards(): pl.pallas_call(project_kernel, grid=(tile // chunk,), in_specs=[pl.BlockS...]
    psum x2 -> x0, blocking collectives: 16.4 us -> none  [the longest x1 9.52 us: shards(): lax.psum(jnp.sum(hidden, axis=-1).astype(jnp.bfloat16), 'ch')]
  transfers between devices with their start and end apart: 3 -> 0, of which waited for: 3 -> 0; matrix products, arithmetic and copies ran while one was open for 1% -> 0% of each run, Pallas kernels for 0% -> 0%
where the time goes in v1:
time: 116 us; the launch traced here: 115 us
  blocking collectives  89.6 us (77%)
  Pallas kernels  18 us (16%)
  local copies, waits for them, and re-layouts  7.48 us (6%)
    all_to_all x1, blocking collectives, shards(): received = lax.all_to_all(message, ('row', 'col'), 0, 0, tiled=True)  56.8 us
    all_to_all x1, blocking collectives, shards(): lax.all_to_all(hidden.reshape(rows * cols * ch, half, lanes), ('row', 'co...  32.8 us
    pallas_call x1, Pallas kernels, shards(): pl.pallas_call(project_kernel, grid=(tile // chunk,), in_specs=[pl.BlockS...  8.74 us
    unnamed x16, local copies, waits for them, and re-layouts  7.48 us
    pallas_call x1, Pallas kernels, shards(): pl.pallas_call(finish_kernel, grid=(groups,), in_specs=[pl.BlockSpec((cha...  5.81 us
    pallas_call x1, Pallas kernels, shards(): pl.pallas_call(product_kernel, grid=(rows // pairs,), in_specs=[pl.BlockS...  3.45 us

profile of v1, /device:TPU:1, one launch (start us, length us, event | category | flops | bytes accessed | tf_op | source)
XLA Modules:
  0.0 115.2 jit_solution(7326972818273260654)
XLA Ops:
  0.0 0.8 copy.11.left_gate_ref
  0.8 0.8 copy.12.left_proj_ref
  1.7 0.8 copy.13.right_gate_ref
  2.5 0.8 copy.14.right_proj_ref
  3.3 0.0 copy-start
  3.3 1.9 %copy-done = bf16[112,112,128]{2,1,0:T(8,128)(2,1)S(1)} copy-done((bf16[112,112,128]{2,1,0:T(8,128)(2,1)S(1)}, bf16[112,112,128]{2,1,0:T(8,128)(2,1)}, u32[]{:S(2)}) %copy-start) | copy-done | bytes 3211288
  5.3 0.0 copy-start.1
  5.3 0.8 copy-done.1
  6.1 0.0 copy-start.2
  6.1 0.8 copy-done.2
  6.8 0.0 copy-start.4
  6.8 0.7 copy-done.4
  7.5 8.7 %project.1 = (bf16[64,2,112,128]{3,2,1,0:T(8,128)(2,1)S(1)}, f32[112,7,8,128]{3,2,1,0:T(8,128)S(1)}) custom-call(bf16[112,112,128]{2,1,0:T(8,128)(2,1)S(1)} %copy-done, s32[112,112]{1,0:T(8,128)S(1)} %copy-done.1, f32[1,128]{1,0:T(1,128)S(1)} %bitcast.10, bf16[128,64]{1,0:T(8,128)(2,1)S(1)} %copy.11.left_gate_ref, bf16[128,64]{1,0:T(8,128)(2,1)S(1)} %copy.12.left_proj_ref, ...), custom_call_target="tpu_custom_call" | custom-call | tf_op jit(solution)/shard_map/project/pallas_call | solution.py:146
  16.2 56.8 %all_to_all.10 = bf16[64,2,112,128]{3,2,1,0:T(8,128)(2,1)S(1)} all-to-all(bf16[64,2,112,128]{3,2,1,0:T(8,128)(2,1)S(1)} %get-tuple-element.7), channel_id=1, replica_groups=mesh['row'=8,'col'=8,'ch'=2] {'row','col'}, dimensions={0} | all-to-all | bytes 7340032 | tf_op jit(solution)/shard_map/all_to_all | solution.py:186
  73.1 3.4 %product.1 = bf16[8,896,128]{2,1,0:T(8,128)(2,1)S(1)} custom-call(bf16[8,8,2,112,128]{4,3,2,1,0:T(8,128)(2,1)S(1)} %bitcast.6, bf16[8,8,2,112,128]{4,3,2,1,0:T(8,128)(2,1)S(1)} %bitcast.7), custom_call_target="tpu_custom_call" | custom-call | tf_op jit(solution)/shard_map/product/pallas_call | solution.py:190
  76.5 0.0 copy-start.3
  76.5 0.0 copy-start.5
  76.6 32.8 %all_to_all.11 = bf16[128,56,128]{2,1,0:T(8,128)(2,1)S(1)} all-to-all(bf16[128,56,128]{2,1,0:T(8,128)(2,1)S(1)} %bitcast.9), channel_id=1, replica_groups=mesh['row'=8,'col'=8,'ch'=2] {'row','col','ch'}, dimensions={0} | all-to-all | bytes 3670016 | tf_op jit(solution)/shard_map/all_to_all | solution.py:204
  109.3 0.0 copy-done.3
  109.3 0.0 copy-done.5
  109.3 5.8 %finish.1 = bf16[112,7,8,128]{3,2,1,0:T(8,128)(2,1)} custom-call(bf16[128,7,8,128]{3,2,1,0:T(8,128)(2,1)S(1)} %bitcast.8, f32[112,7,8,128]{3,2,1,0:T(8,128)S(1)} %get-tuple-element.8.gate_ref, f32[1,128]{1,0:T(1,128)S(1)} %bitcast.11, bf16[128,128]{1,0:T(8,128)(2,1)S(1)} %copy-done.3), custom_call_target="tpu_custom_call" | custom-call | tf_op jit(solution)/shard_map/finish/pallas_call | solution.py:209
Async XLA Ops:
  3.3 1.9 %copy-start = (bf16[112,112,128]{2,1,0:T(8,128)(2,1)S(1)}, bf16[112,112,128]{2,1,0:T(8,128)(2,1)}, u32[]{:S(2)}) copy-start(bf16[112,112,128]{2,1,0:T(8,128)(2,1)} %pair_ref.1) | copy-start | bytes 9633796
  5.3 0.8 copy-start.1
  6.1 0.8 copy-start.2
  6.8 0.7 copy-start.4
  76.5 32.8 %copy-start.3 = (bf16[128,128]{1,0:T(8,128)(2,1)S(1)}, bf16[128,128]{1,0:T(8,128)(2,1)}, u32[]{:S(2)}) copy-start(bf16[128,128]{1,0:T(8,128)(2,1)} %weight_ref.1) | copy-start | bytes 98308
  76.5 32.8 %copy-start.5 = (f32[128]{0:T(128)S(1)}, f32[128]{0:T(128)}, u32[]{:S(2)}) copy-start(f32[128]{0:T(128)} %param.18) | copy-start | bytes 1540

commit v2 on v1

--- a/solution.py
+++ b/solution.py
@@ -14,6 +14,12 @@
 
 def sigmoid(values):
     return 0.5 * jnp.tanh(0.5 * values) + 0.5
+
+
+def normalize(values, gain):
+    centered = values - jnp.mean(values, axis=-1, keepdims=True)
+    spread = jnp.mean(centered * centered, axis=-1, keepdims=True)
+    return centered * lax.rsqrt(spread + epsilon) * gain
 
 
 def project_kernel(
@@ -24,39 +30,25 @@
     left_proj_ref,
     right_gate_ref,
     right_proj_ref,
-    gate_weight_ref,
     message_ref,
-    gate_ref,
     weight_scr,
     normed_scr,
     mask_scr,
     turn_scr,
 ):
     tile = pair_ref.shape[1]
-    part = left_gate_ref.shape[1]
-    half = tile // 2
+    part = left_gate_ref.shape[0]
 
     @pl.when(pl.program_id(0) == 0)
     def _():
-        joined = jnp.concatenate(
-            [left_gate_ref[...], left_proj_ref[...], right_gate_ref[...], right_proj_ref[...]],
-            axis=1,
-        )
-        weight_scr[...] = joined.astype(f32).T.astype(bf16)
+        for place, ref in enumerate((left_gate_ref, left_proj_ref, right_gate_ref, right_proj_ref)):
+            weight_scr[place * part : (place + 1) * part, :] = ref[...] * 0.5
         normed_scr[...] = jnp.zeros_like(normed_scr)
         mask_scr[...] = jnp.zeros_like(mask_scr)
 
-    values = pair_ref[...].astype(f32)
-    centered = values - jnp.mean(values, axis=-1, keepdims=True)
-    spread = jnp.mean(centered * centered, axis=-1, keepdims=True)
-    normed = centered * lax.rsqrt(spread + epsilon) * gain_ref[...][None]
+    normed = normalize(pair_ref[...].astype(f32), gain_ref[...][None])
     normed_scr[:, :tile, :] = normed.astype(bf16)
     mask_scr[:, :tile] = mask_ref[...].astype(f32)
-
-    own = jnp.where(lax.axis_index("ch") == 0, normed[:, :half], normed[:, half:])
-    own = own.reshape(chunk * half, lanes).astype(bf16)
-    gate = sigmoid(jnp.dot(own, gate_weight_ref[...], preferred_element_type=f32))
-    gate_ref[...] = gate.reshape(gate_ref.shape)
 
     for k in range(0, chunk, 2):
         source = normed_scr[k : k + 2].reshape(2 * lanes, lanes)
@@ -69,13 +61,22 @@
             for side in range(2):
                 base = 2 * part * side
                 vals = (
-                    valid
-                    * sigmoid(own_lanes[base : base + part])
+                    (jnp.tanh(own_lanes[base : base + part]) + 1.0)
                     * own_lanes[base + part : base + 2 * part]
+                    * valid
                 )
                 turn_scr[side, pl.ds(k + kk, part, stride=chunk), :] = vals
     for side in range(2):
         message_ref[:, side] = turn_scr[side].reshape(part, chunk, lanes).astype(bf16)
+
+
+def gate_kernel(pair_ref, gain_ref, weight_ref, gate_ref):
+    half = pair_ref.shape[1] // 2
+    values = pair_ref[...].astype(f32)
+    own = jnp.where(lax.axis_index("ch") == 0, values[:, :half], values[:, half:])
+    normed = normalize(own, gain_ref[...][None]).reshape(chunk * half, lanes).astype(bf16)
+    gate = jnp.dot(normed, weight_ref[...], preferred_element_type=f32)
+    gate_ref[...] = sigmoid(gate).reshape(gate_ref.shape)
 
 
 def product_kernel(left_ref, right_ref, out_ref, right_scr):
@@ -143,27 +144,24 @@
     groups = half // 8
     whole = lambda shape: pl.BlockSpec(shape, lambda s: (0,) * len(shape))
 
-    message, gate = pl.pallas_call(
+    stay = lambda array: pltpu.with_memory_space_constraint(array, pltpu.HBM)
+    pair = stay(pair)
+    gain_row = stay(ln_in_gain.reshape(1, channels))
+    weights = [stay(w.T) for w in (w_left_gate, w_left_proj, w_right_gate, w_right_proj)]
+    message = pl.pallas_call(
         project_kernel,
         grid=(tile // chunk,),
         in_specs=[
             pl.BlockSpec((chunk, tile, channels), lambda s: (s, 0, 0)),
             pl.BlockSpec((chunk, tile), lambda s: (s, 0)),
             whole((1, channels)),
-            whole((channels, part)),
-            whole((channels, part)),
-            whole((channels, part)),
-            whole((channels, part)),
-            whole((channels, channels)),
-        ],
-        out_specs=[
-            pl.BlockSpec((part, 2, chunk, lanes), lambda s: (0, 0, s, 0)),
-            pl.BlockSpec((chunk, groups, 8, lanes), lambda s: (s, 0, 0, 0)),
-        ],
-        out_shape=[
-            jax.ShapeDtypeStruct((part, 2, tile, lanes), bf16),
-            jax.ShapeDtypeStruct((tile, groups, 8, lanes), f32),
-        ],
+            whole((part, channels)),
+            whole((part, channels)),
+            whole((part, channels)),
+            whole((part, channels)),
+        ],
+        out_specs=pl.BlockSpec((part, 2, chunk, lanes), lambda s: (0, 0, s, 0)),
+        out_shape=jax.ShapeDtypeStruct((part, 2, tile, lanes), bf16),
         scratch_shapes=[
             pltpu.VMEM((4 * part, channels), bf16),
             pltpu.VMEM((chunk, lanes, channels), bf16),
@@ -172,16 +170,26 @@
         ],
         compiler_params=pltpu.CompilerParams(vmem_limit_bytes=24 * 2**20),
         name="project",
-    )(
-        pair,
-        pair_mask,
-        ln_in_gain.reshape(1, channels),
-        w_left_gate,
-        w_left_proj,
-        w_right_gate,
-        w_right_proj,
-        w_gate,
-    )
+    )(pair, stay(pair_mask), gain_row, *weights)
+
+    gate = pl.pallas_call(
+        gate_kernel,
+        grid=(tile // chunk,),
+        in_specs=[
+            pl.BlockSpec((chunk, tile, channels), lambda s: (s, 0, 0)),
+            whole((1, channels)),
+            whole((channels, channels)),
+        ],
+        out_specs=pl.BlockSpec((chunk, groups, 8, lanes), lambda s: (s, 0, 0, 0)),
+        out_shape=jax.ShapeDtypeStruct((tile, groups, 8, lanes), f32),
+        compiler_params=pltpu.CompilerParams(vmem_limit_bytes=24 * 2**20),
+        cost_estimate=pl.CostEstimate(
+            flops=2 * tile * half * channels * channels,
+            bytes_accessed=10 * tile * half * channels,
+            transcendentals=tile * half * channels,
+        ),
+        name="gate",
+    )(pair, gain_row, stay(w_gate))
 
     received = lax.all_to_all(message, ("row", "col"), 0, 0, tiled=True)
     received = received.reshape(rows, cols, 2, tile, lanes)
@@ -224,7 +232,7 @@
         ],
         compiler_params=pltpu.CompilerParams(vmem_limit_bytes=24 * 2**20),
         name="finish",
-    )(parts, gate, ln_out_gain.reshape(1, channels), w_out)
+    )(parts, gate, stay(ln_out_gain.reshape(1, channels)), stay(w_out))
     return update.reshape(tile, half, channels)
 
 

time: 116 us -> 112 us (0.966)
  blocking collectives: 89.6 us -> 56.8 us
  waiting for transfers between devices: 0 us -> 21.6 us
  Pallas kernels: 18 us -> 27.3 us
  local copies, waits for them, and re-layouts: 7.48 us -> 0 us
  starting transfers between devices: 0 us -> 5.49 us
    all_to_all x1 -> x0, blocking collectives: 32.8 us -> none  [shards(): lax.all_to_all(hidden.reshape(rows * cols * ch, half, lanes), ('row', 'co...]
    all_to_all x0 -> x1, waiting for transfers between devices: none -> 21.6 us  [shards(): lax.all_to_all(hidden.reshape(rows * cols * ch, half, lanes), ('row', 'co...]
    unnamed x16 -> x0, local copies, waits for them, and re-layouts: 7.48 us -> none
    pallas_call x0 -> x1, Pallas kernels: none -> 5.98 us  [shards(): pl.pallas_call(gate_kernel, grid=(tile // chunk,), in_specs=[pl.BlockSpec...]
    all_to_all x0 -> x1, starting transfers between devices: none -> 5.49 us  [shards(): lax.all_to_all(hidden.reshape(rows * cols * ch, half, lanes), ('row', 'co...]
    pallas_call x1, Pallas kernels: 5.81 us -> 7.41 us  [shards(): pl.pallas_call(finish_kernel, grid=(groups,), in_specs=[pl.BlockSpec((cha...]
  transfers between devices with their start and end apart: 0 -> 1, of which waited for: 0 -> 1; matrix products, arithmetic and copies ran while one was open for 0% -> 0% of each run, Pallas kernels for 0% -> 5%
where the time goes in v2:
time: 112 us; the launch traced here: 111 us
  blocking collectives  56.8 us (51%)
  Pallas kernels  27.3 us (24%)
  waiting for transfers between devices  21.6 us (19%)
  starting transfers between devices  5.49 us (5%)
    all_to_all x1, blocking collectives, shards(): received = lax.all_to_all(message, ('row', 'col'), 0, 0, tiled=True)  56.8 us
    all_to_all x1, waiting for transfers between devices, shards(): lax.all_to_all(hidden.reshape(rows * cols * ch, half, lanes), ('row', 'co...  21.6 us
    pallas_call x1, Pallas kernels, shards(): pl.pallas_call(project_kernel, grid=(tile // chunk,), in_specs=[pl.BlockS...  9.65 us
    pallas_call x1, Pallas kernels, shards(): pl.pallas_call(finish_kernel, grid=(groups,), in_specs=[pl.BlockSpec((cha...  7.41 us
    pallas_call x1, Pallas kernels, shards(): pl.pallas_call(gate_kernel, grid=(tile // chunk,), in_specs=[pl.BlockSpec...  5.98 us
    all_to_all x1, starting transfers between devices, shards(): lax.all_to_all(hidden.reshape(rows * cols * ch, half, lanes), ('row', 'co...  5.49 us
    pallas_call x1, Pallas kernels, shards(): pl.pallas_call(product_kernel, grid=(rows // pairs,), in_specs=[pl.BlockS...  4.27 us
  transfers between devices with their start and end apart: 1, of which 1 were waited for; matrix products, arithmetic and copies ran while one was open for 0% of the time, Pallas kernels for 5%

profile of v2, /device:TPU:1, one launch (start us, length us, event | category | flops | bytes accessed | tf_op | source)
XLA Modules:
  0.0 111.3 jit_solution(4741945741655277133)
XLA Ops:
  0.0 9.7 %project.1 = bf16[64,2,112,128]{3,2,1,0:T(8,128)(2,1)S(1)} custom-call(bf16[112,112,128]{2,1,0:T(8,128)(2,1)} %pair_ref.3, s32[112,112]{1,0:T(8,128)} %mask_ref.1, f32[1,128]{1,0:T(1,128)} %bitcast.16, bf16[64,128]{1,0:T(8,128)(2,1)} %bitcast.12, bf16[64,128]{1,0:T(8,128)(2,1)} %bitcast.13, bf16[64,128]{1,0:T(8,128)(2,1)} %bitcast.14, bf16[64,128]{1,0:T(8,128)(2,1)} %bitcast.15), custom_call_target="tpu_custom_call" | custom-call | tf_op jit(solution)/shard_map/project/pallas_call | solution.py:151
  9.7 56.8 %all_to_all.10 = bf16[64,2,112,128]{3,2,1,0:T(8,128)(2,1)S(1)} all-to-all(bf16[64,2,112,128]{3,2,1,0:T(8,128)(2,1)S(1)} %project.1), channel_id=1, replica_groups=mesh['row'=8,'col'=8,'ch'=2] {'row','col'}, dimensions={0} | all-to-all | bytes 7340032 | tf_op jit(solution)/shard_map/all_to_all | solution.py:194
  66.5 4.3 %product.1 = bf16[8,896,128]{2,1,0:T(8,128)(2,1)} custom-call(bf16[8,8,2,112,128]{4,3,2,1,0:T(8,128)(2,1)S(1)} %bitcast.10, bf16[8,8,2,112,128]{4,3,2,1,0:T(8,128)(2,1)S(1)} %bitcast.11), custom_call_target="tpu_custom_call" | custom-call | tf_op jit(solution)/shard_map/product/pallas_call | solution.py:198
  70.8 5.5 %all-to-all-start.1 = ((bf16[128,56,128]{2,1,0:T(8,128)(2,1)}), bf16[128,56,128]{2,1,0:T(8,128)(2,1)}, u32[]{:S(2)}, u32[]{:S(2)}) async-start(bf16[128,56,128]{2,1,0:T(8,128)(2,1)} %bitcast.6), calls=%async_computation.1 | async-start | bytes 3670016 | tf_op jit(solution)/shard_map/all_to_all | solution.py:212
  76.3 6.0 %gate.1.gate_ref = f32[112,7,8,128]{3,2,1,0:T(8,128)S(1)} custom-call(bf16[112,112,128]{2,1,0:T(8,128)(2,1)} %pair_ref.3, f32[1,128]{1,0:T(1,128)} %bitcast.17, bf16[128,128]{1,0:T(8,128)(2,1)} %weight_ref.2), custom_call_target="tpu_custom_call" | custom-call | flops 205520896 | bytes 8028160 | tf_op jit(solution)/shard_map/gate/pallas_call | solution.py:175
  82.3 21.6 %all-to-all-done.1 = bf16[128,56,128]{2,1,0:T(8,128)(2,1)} async-done(((bf16[128,56,128]{2,1,0:T(8,128)(2,1)}), bf16[128,56,128]{2,1,0:T(8,128)(2,1)}, u32[]{:S(2)}, u32[]{:S(2)}) %all-to-all-start.1) | async-done | bytes 1835040 | tf_op jit(solution)/shard_map/all_to_all | solution.py:212
  103.9 7.4 %finish.1 = bf16[112,7,8,128]{3,2,1,0:T(8,128)(2,1)} custom-call(bf16[128,7,8,128]{3,2,1,0:T(8,128)(2,1)} %bitcast.7.hidden_ref, f32[112,7,8,128]{3,2,1,0:T(8,128)S(1)} %gate.1.gate_ref, f32[1,128]{1,0:T(1,128)} %bitcast.18, bf16[128,128]{1,0:T(8,128)(2,1)} %weight_ref.3), custom_call_target="tpu_custom_call" | custom-call | tf_op jit(solution)/shard_map/finish/pallas_call | solution.py:217
Async XLA Ops:
  70.8 33.1 %all-to-all-start.1 = ((bf16[128,56,128]{2,1,0:T(8,128)(2,1)}), bf16[128,56,128]{2,1,0:T(8,128)(2,1)}, u32[]{:S(2)}, u32[]{:S(2)}) async-start(bf16[128,56,128]{2,1,0:T(8,128)(2,1)} %bitcast.6), calls=%async_computation.1 | async-start | bytes 3670016 | tf_op jit(solution)/shard_map/all_to_all | solution.py:212

commit v3 on v2

v3 whole, which is shorter than its diff:
```python
import jax
import jax.numpy as jnp
from jax import lax
from jax.experimental import pallas as pl
from jax.experimental.pallas import tpu as pltpu
from jax.sharding import PartitionSpec as P

epsilon = 1e-05
f32 = jnp.float32
bf16 = jnp.bfloat16
lanes = 128
chunk = 16
turned = (((1,), (1,)), ((), ()))

edge = 96
spill = 24


def project_kernel(
    pair_hbm,
    mask_ref,
    gain_ref,
    left_gate_ref,
    left_proj_ref,
    right_gate_ref,
    right_proj_ref,
    message_ref,
    pair_scr,
    weight_scr,
    center_scr,
    mask_scr,
    normed_a,
    normed_b,
    upper_a,
    upper_b,
    lower_a,
    lower_b,
    spill_scr,
    sems,
):
    tile = pair_hbm.shape[0]
    part = left_gate_ref.shape[0]
    count = tile // chunk
    order = (count - 1, count - 2) + tuple(range(count - 2))
    normed_refs, uppers, lowers = (normed_a, normed_b), (upper_a, upper_b), (lower_a, lower_b)

    def fetch(c):
        rows = pl.ds(c * chunk, chunk)
        return pltpu.make_async_copy(pair_hbm.at[rows], pair_scr.at[rows], sems.at[c])

    for c in order:
        fetch(c).start()
    gain = gain_ref[...] * 0.5
    for place, ref in enumerate((left_gate_ref, left_proj_ref, right_gate_ref, right_proj_ref)):
        weight_scr[place * part : (place + 1) * part, :] = (ref[...].astype(f32) * gain).astype(bf16)
    rows = lax.broadcasted_iota(jnp.int32, (lanes, lanes), 0)
    cols = lax.broadcasted_iota(jnp.int32, (lanes, lanes), 1)
    center_scr[...] = (jnp.where(rows == cols, 1.0, 0.0) - 1.0 / lanes).astype(bf16)
    mask = mask_ref[...].astype(f32)
    mask_scr[...] = jnp.concatenate([mask, mask[:, edge:]], axis=1)
    lane = lax.broadcasted_iota(jnp.int32, (1, lanes), 1)
    middle = (lane >= edge) & (lane < tile)
    spill_scr[:, 9 * 8 :, :] = jnp.zeros((part, 8, lanes), f32)

    def norm(c, k, normed_ref):
        first, second = pair_scr[c * chunk + k], pair_scr[c * chunk + k + 1]
        source = jnp.concatenate([first, first[edge:], second, second[edge:]], axis=0)
        centered = lax.dot_general(center_scr[...], source, turned, preferred_element_type=f32)
        spread = jnp.sum(centered * centered, axis=0, keepdims=True) * (1.0 / lanes)
        normed_ref[k // 2] = (centered * lax.rsqrt(spread + epsilon)).astype(bf16)

    def values(c, k, normed_ref, upper, lower):
        normed = normed_ref[k // 2]
        left = jnp.dot(weight_scr[: 2 * part], normed, preferred_element_type=f32)
        right = jnp.dot(weight_scr[2 * part :], normed, preferred_element_type=f32)
        for kk in range(2):
            own = slice(kk * lanes, (kk + 1) * lanes)
            row = k + kk
            valid = mask_scr[c * chunk + row : c * chunk + row + 1, :]
            left_vals = (jnp.tanh(left[:part, own]) + 1.0) * left[part:, own] * valid
            right_vals = (jnp.tanh(right[:part, own]) + 1.0) * right[part:, own] * valid
            place = pl.ds(row % 8, part, stride=8)
            upper[row // 8, place, :] = jnp.where(middle, right_vals, left_vals)
            lower[row // 8, place, :] = right_vals

    def store(c, ch, upper, lower):
        def eight(ref, half):
            return ref[half, ch * 8 : (ch + 8) * 8].reshape(8, 8, lanes)

        own = slice(ch, ch + 8)
        at = c * chunk
        message_ref[own, at : at + chunk, :] = jnp.concatenate(
            [eight(upper, 0), eight(upper, 1)], axis=1
        ).astype(bf16)

        def keep(p, half):
            rows = eight(lower, half).reshape(64, lanes)
            for s in range(3):
                to = 8 * (3 * p + s)
                moved = pltpu.roll(rows, edge - 32 * s, 1)
                spill_scr[own, to : to + 8, :] = moved.reshape(8, 8, lanes)

        if c == count - 1:
            keep(1, 0)
            keep(2, 1)
        elif c == count - 2:
            keep(0, 1)
            message_ref[own, tile + at : tile + at + 8, :] = eight(lower, 0).astype(bf16)
        else:
            rows = jnp.concatenate([eight(lower, 0), eight(lower, 1)], axis=1)
            rows = jnp.where(lane[None] < edge, rows, spill_scr[own, at : at + chunk, :])
            message_ref[own, tile + at : tile + at + chunk, :] = rows.astype(bf16)

    for step in range(count + 2):
        if step < count:
            fetch(order[step]).wait()
        for k in range(0, chunk, 2):
            if step < count:
                norm(order[step], k, normed_refs[step % 2])
            if 1 <= step < count + 1:
                last = (step - 1) % 2
                values(order[step - 1], k, normed_refs[last], uppers[last], lowers[last])
            if 2 <= step:
                store(order[step - 2], k * part // chunk, uppers[step % 2], lowers[step % 2])


def normalize(values, gain):
    centered = values - jnp.mean(values, axis=-1, keepdims=True)
    spread = jnp.mean(centered * centered, axis=-1, keepdims=True)
    return centered * lax.rsqrt(spread + epsilon) * gain


def sigmoid(values):
    return 0.5 * jnp.tanh(0.5 * values) + 0.5


def gate_kernel(pair_ref, gain_ref, weight_ref, gate_ref):
    half = pair_ref.shape[1] // 2
    values = pair_ref[...].astype(f32)
    own = jnp.where(lax.axis_index("ch") == 0, values[:, :half], values[:, half:])
    normed = normalize(own, gain_ref[...][None]).reshape(chunk * half, lanes).astype(bf16)
    gate = jnp.dot(normed, weight_ref[...], preferred_element_type=f32)
    gate_ref[...] = sigmoid(gate).reshape(gate_ref.shape)


def product_kernel(received_ref, out_hbm, right_a, right_b, out_scr, sems):
    rows, half_cols, tile = 8, 4, received_ref.shape[1] - 88
    cols, steps = 2 * half_cols, rows // 2
    rights = (right_a, right_b)
    lane = lax.broadcasted_iota(jnp.int32, (1, lanes), 1)

    def turn(q):
        blocks = []
        for r in range(rows):
            upper = received_ref[r * cols + q, :tile].astype(f32)
            lower = received_ref[r * cols + q, tile:].astype(f32)
            parts = [jnp.where(lane < edge, lower, upper[: tile - spill])]
            for p in range(3):
                pieces = [
                    pltpu.roll(lower[8 * (3 * p + s) : 8 * (3 * p + s) + 8], 32 * s + 32, 1)
                    for s in range(3)
                ]
                at = tile - spill + 8 * p
                eight = jnp.where(lane < edge, pieces[2], upper[at : at + 8])
                eight = jnp.where(lane < 64, pieces[1], eight)
                parts.append(jnp.where(lane < 32, pieces[0], eight))
            blocks.append(jnp.concatenate(parts, axis=0).astype(bf16))
        block = jnp.concatenate(blocks, axis=0)
        at = (q % half_cols) * tile
        rights[q // half_cols][at : at + tile, :] = block.T[:tile]

    def send(s, h):
        width = half_cols * tile
        return pltpu.make_async_copy(
            out_scr.at[s, h], out_hbm.at[pl.ds(2 * s, 2), pl.ds(h * width, width)], sems.at[s, h]
        )

    def multiply(s, h):
        lefts = [
            jnp.concatenate([received_ref[r * cols + 2 * s + p, :tile] for r in range(rows)], axis=0)
            for p in range(2)
        ]
        hidden = jnp.dot(
            rights[h][...], jnp.concatenate(lefts, axis=1), preferred_element_type=f32
        ).astype(bf16)
        for p in range(2):
            out_scr[s, h, p] = hidden[:, p * lanes : (p + 1) * lanes]
        send(s, h).start()

    for q in range(half_cols):
        turn(q)
    for s in range(steps):
        turn(half_cols + s)
        multiply(s, 0)
    for s in range(steps):
        multiply(s, 1)
    for s in range(steps):
        for h in range(2):
            send(s, h).wait()


def finish_kernel(
    hidden_hbm,
    gate_hbm,
    gain_ref,
    weight_ref,
    out_hbm,
    hidden_scr,
    gate_scr,
    out_scr,
    weight_scr,
    turn_a,
    turn_b,
    part_a,
    part_b,
    hidden_sems,
    gate_sems,
    out_sems,
):
    groups, channels, tile = hidden_scr.shape[0], hidden_scr.shape[1], out_scr.shape[1]
    turns, outs = (turn_a, turn_b), (part_a, part_b)
    step = 16

    def fetch_hidden(g):
        return pltpu.make_async_copy(hidden_hbm.at[:, g], hidden_scr.at[g], hidden_sems.at[g])

    def fetch_gate(g):
        return pltpu.make_async_copy(gate_hbm.at[:, g], gate_scr.at[g], gate_sems.at[g])

    def send(g):
        return pltpu.make_async_copy(out_scr.at[g], out_hbm.at[:, g], out_sems.at[g])

    for g in range(groups):
        fetch_hidden(g).start()
    for g in range(groups):
        fetch_gate(g).start()
    scaled = jnp.broadcast_to(gain_ref[...], (channels, channels)).T * weight_ref[...].astype(f32)
    part = channels // 2
    for side in range(2):
        turn_a[pl.ds(side, part, stride=2), :] = scaled[side * part : (side + 1) * part]
    weight_scr[...] = turn_a[:channels, :].astype(bf16)

    def tree(terms):
        while len(terms) > 1:
            terms = [terms[n] + terms[n + 1] for n in range(0, len(terms), 2)]
        return terms[0]

    def norm(g):
        def block(c):
            return hidden_scr[g, c : c + step].astype(f32)

        starts = range(0, channels, step)
        center = tree([jnp.sum(block(c), axis=0) for c in starts]) * (1.0 / channels)
        squares = []
        for c in starts:
            centered = block(c) - center[None]
            squares.append(jnp.sum(centered * centered, axis=0))
        scale = lax.rsqrt(tree(squares) * (1.0 / channels) + epsilon)
        for c in starts:
            normed = (block(c) - center[None]) * scale[None]
            turns[g % 2][c * 8 : (c + step) * 8] = normed.reshape(step * 8, lanes)

    def project(g, j):
        row = turns[g % 2][pl.ds(j, channels, stride=8), :].astype(bf16)
        projected = lax.dot_general(
            row, weight_scr[...], (((0,), (0,)), ((), ())), preferred_element_type=f32
        )
        outs[g % 2][pl.ds(j, edge, stride=8), :] = projected[:edge]
        outs[g % 2][pl.ds(edge * 8 + j, tile - edge, stride=8), :] = projected[tile:]

    def multiply(g, n):
        count = tile // 8
        own = slice(n * count, (n + 1) * count)
        rows = outs[g % 2][n * count * 8 : (n + 1) * count * 8].reshape(count, 8, lanes)
        out_scr[g, own] = (rows * gate_scr[g, own]).astype(bf16)

    for s in range(groups + 2):
        if s < groups:
            fetch_hidden(s).wait()
        if 2 <= s:
            fetch_gate(s - 2).wait()
        if s < groups:
            norm(s)
        for j in range(8):
            if 2 <= s:
                multiply(s - 2, j)
            if 1 <= s < groups + 1:
                project(s - 1, j)
        if 2 <= s:
            send(s - 2).start()
    for g in range(groups):
        send(g).wait()


def shards(
    pair,
    pair_mask,
    ln_in_gain,
    w_left_gate,
    w_left_proj,
    w_right_gate,
    w_right_proj,
    w_gate,
    ln_out_gain,
    w_out,
):
    tile, channels = pair.shape[0], pair.shape[2]
    part = w_left_gate.shape[1]
    rows, cols, ch = lax.axis_size("row"), lax.axis_size("col"), lax.axis_size("ch")
    half = tile // ch
    groups = half // 8
    limit = pltpu.CompilerParams(vmem_limit_bytes=24 * 2**20)
    vmem, anywhere = pl.BlockSpec(memory_space=pltpu.VMEM), pl.BlockSpec(memory_space=pl.ANY)
    whole = lambda shape: pl.BlockSpec(shape, lambda s: (0,) * len(shape))

    stay = lambda array: pltpu.with_memory_space_constraint(array, pltpu.HBM)
    pair = stay(pair)
    gain_row = stay(ln_in_gain.reshape(1, channels))
    weights = [stay(w.T) for w in (w_left_gate, w_left_proj, w_right_gate, w_right_proj)]
    normed_shape = pltpu.VMEM((chunk // 2, channels, 2 * lanes), bf16)
    turn_shape = pltpu.VMEM((2, part * 8, lanes), f32)
    message = pl.pallas_call(
        project_kernel,
        in_specs=[anywhere] + [vmem] * 6,
        out_specs=vmem,
        out_shape=jax.ShapeDtypeStruct((part, 2 * tile - spill, lanes), bf16),
        scratch_shapes=[
            pltpu.VMEM(pair.shape, bf16),
            pltpu.VMEM((4 * part, channels), bf16),
            pltpu.VMEM((channels, channels), bf16),
            pltpu.VMEM((tile, lanes), f32),
            normed_shape,
            normed_shape,
            turn_shape,
            turn_shape,
            turn_shape,
            turn_shape,
            pltpu.VMEM((part, 80, lanes), f32),
            pltpu.SemaphoreType.DMA((tile // chunk,)),
        ],
        compiler_params=limit,
        name="project",
    )(pair, stay(pair_mask), gain_row, *weights)

    gate = pl.pallas_call(
        gate_kernel,
        grid=(tile // chunk,),
        in_specs=[
            pl.BlockSpec((chunk, tile, channels), lambda s: (s, 0, 0)),
            whole((1, channels)),
            whole((channels, channels)),
        ],
        out_specs=pl.BlockSpec((chunk, groups, 8, lanes), lambda s: (s, 0, 0, 0)),
        out_shape=jax.ShapeDtypeStruct((tile, groups, 8, lanes), f32),
        compiler_params=limit,
        cost_estimate=pl.CostEstimate(
            flops=2 * tile * half * channels * channels,
            bytes_accessed=10 * tile * half * channels,
            transcendentals=tile * half * channels,
        ),
        name="gate",
    )(pair, gain_row, stay(w_gate))

    received = lax.all_to_all(message, ("row", "col"), 0, 0, tiled=True)

    hidden = pl.pallas_call(
        product_kernel,
        in_specs=[vmem],
        out_specs=anywhere,
        out_shape=jax.ShapeDtypeStruct((rows, cols * tile, lanes), bf16),
        scratch_shapes=[
            pltpu.VMEM((cols * tile // 2, rows * tile), bf16),
            pltpu.VMEM((cols * tile // 2, rows * tile), bf16),
            pltpu.VMEM((rows // 2, 2, 2, cols * tile // 2, lanes), bf16),
            pltpu.SemaphoreType.DMA((rows // 2, 2)),
        ],
        compiler_params=limit,
        name="product",
    )(received)

    parts = lax.all_to_all(
        hidden.reshape(rows * cols * ch, half, lanes), ("row", "col", "ch"), 0, 0, tiled=True
    )
    parts = parts.reshape(channels, groups, 8, lanes)

    update = pl.pallas_call(
        finish_kernel,
        in_specs=[anywhere, anywhere, vmem, vmem],
        out_specs=anywhere,
        out_shape=jax.ShapeDtypeStruct((tile, groups, 8, lanes), bf16),
        scratch_shapes=[
            pltpu.VMEM((groups, channels, 8, lanes), bf16),
            pltpu.VMEM((groups, tile, 8, lanes), f32),
            pltpu.VMEM((groups, tile, 8, lanes), bf16),
            pltpu.VMEM((channels, channels), bf16),
            pltpu.VMEM((channels * 8, lanes), f32),
            pltpu.VMEM((channels * 8, lanes), f32),
            pltpu.VMEM((tile * 8, lanes), f32),
            pltpu.VMEM((tile * 8, lanes), f32),
            pltpu.SemaphoreType.DMA((groups,)),
            pltpu.SemaphoreType.DMA((groups,)),
            pltpu.SemaphoreType.DMA((groups,)),
        ],
        compiler_params=limit,
        name="finish",
    )(parts, gate, ln_out_gain.reshape(1, channels), w_out)
    return update.reshape(tile, half, channels)


def solution(mesh):
    in_specs = (
        P("row", "col", None),
        P("row", "col"),
        P(),
        P(None, "ch"),
        P(None, "ch"),
        P(None, "ch"),
        P(None, "ch"),
        P(),
        P(),
        P(),
    )
    out_specs = P("row", ("col", "ch"), None)
    return jax.shard_map(shards, mesh=mesh, in_specs=in_specs, out_specs=out_specs, check_vma=False)
```

time: 112 us -> 102 us (0.911)
  Pallas kernels: 27.3 us -> 21.7 us
  blocking collectives: 56.8 us -> 52.8 us
    pallas_call x3, Pallas kernels: 21.3 us -> 15.8 us  [the longest x1 6.99 us: shards(): pl.pallas_call(project_kernel, in_specs=[anywhere] + [vmem] * 6, out_spec...]
    all_to_all x1, blocking collectives: 56.8 us -> 52.8 us  [shards(): received = lax.all_to_all(message, ('row', 'col'), 0, 0, tiled=True)]
  transfers between devices with their start and end apart: 1 -> 1, of which waited for: 1 -> 1; matrix products, arithmetic and copies ran while one was open for 0% -> 0% of each run, Pallas kernels for 5% -> 6%
where the time goes in v3:
time: 102 us
  blocking collectives  52.8 us (52%)
  Pallas kernels  21.7 us (21%)
  waiting for transfers between devices  21.6 us (21%)
  starting transfers between devices  5.48 us (5%)
    all_to_all x1, blocking collectives, shards(): received = lax.all_to_all(message, ('row', 'col'), 0, 0, tiled=True)  52.8 us
    all_to_all x1, waiting for transfers between devices, shards(): lax.all_to_all(hidden.reshape(rows * cols * ch, half, lanes), ('row', 'co...  21.6 us
    pallas_call x1, Pallas kernels, shards(): pl.pallas_call(project_kernel, in_specs=[anywhere] + [vmem] * 6, out_spec...  6.99 us
    pallas_call x1, Pallas kernels, shards(): pl.pallas_call(gate_kernel, grid=(tile // chunk,), in_specs=[pl.BlockSpec...  5.98 us
    all_to_all x1, starting transfers between devices, shards(): lax.all_to_all(hidden.reshape(rows * cols * ch, half, lanes), ('row', 'co...  5.48 us
    pallas_call x1, Pallas kernels, shards(): pl.pallas_call(finish_kernel, in_specs=[anywhere, anywhere, vmem, vmem],...  4.83 us
    pallas_call x1, Pallas kernels, shards(): pl.pallas_call(product_kernel, in_specs=[vmem], out_specs=anywhere, out_s...  3.94 us
  transfers between devices with their start and end apart: 1, of which 1 were waited for; matrix products, arithmetic and copies ran while one was open for 0% of the time, Pallas kernels for 6%

profile of v3, /device:TPU:1, one launch (start us, length us, event | category | flops | bytes accessed | tf_op | source)
XLA Modules:
  0.0 101.8 jit_solution(8341935917508512623)
XLA Ops:
  0.0 7.0 %project.1 = bf16[64,200,128]{2,1,0:T(8,128)(2,1)S(1)} custom-call(bf16[112,112,128]{2,1,0:T(8,128)(2,1)} %pair_ref.1, s32[112,112]{1,0:T(8,128)} %mask_ref.1, f32[1,128]{1,0:T(1,128)} %bitcast.14, bf16[64,128]{1,0:T(8,128)(2,1)} %bitcast.10, bf16[64,128]{1,0:T(8,128)(2,1)} %bitcast.11, bf16[64,128]{1,0:T(8,128)(2,1)} %bitcast.12, bf16[64,128]{1,0:T(8,128)(2,1)} %bitcast.13), custom_call_target="tpu_custom_call" | custom-call | tf_op jit(solution)/shard_map/project/pallas_call | solution.py:322
  7.0 52.8 %all_to_all.10.received_ref = bf16[64,200,128]{2,1,0:T(8,128)(2,1)S(1)} all-to-all(bf16[64,200,128]{2,1,0:T(8,128)(2,1)S(1)} %project.1), channel_id=1, replica_groups=mesh['row'=8,'col'=8,'ch'=2] {'row','col'}, dimensions={0} | all-to-all | bytes 6553600 | tf_op jit(solution)/shard_map/all_to_all | solution.py:364
  59.8 3.9 %product.1 = bf16[8,896,128]{2,1,0:T(8,128)(2,1)} custom-call(bf16[64,200,128]{2,1,0:T(8,128)(2,1)S(1)} %all_to_all.10.received_ref), custom_call_target="tpu_custom_call" | custom-call | tf_op jit(solution)/shard_map/product/pallas_call | solution.py:366
  63.7 5.5 %all-to-all-start.1 = ((bf16[128,56,128]{2,1,0:T(8,128)(2,1)}), bf16[128,56,128]{2,1,0:T(8,128)(2,1)}, u32[]{:S(2)}, u32[]{:S(2)}) async-start(bf16[128,56,128]{2,1,0:T(8,128)(2,1)} %bitcast.5), calls=%async_computation.1 | async-start | bytes 3670016 | tf_op jit(solution)/shard_map/all_to_all | solution.py:381
  69.2 0.0 copy-start
  69.3 0.0 copy-start.1
  69.3 6.0 %gate.1.gate_hbm = f32[112,7,8,128]{3,2,1,0:T(8,128)S(1)} custom-call(bf16[112,112,128]{2,1,0:T(8,128)(2,1)} %pair_ref.1, f32[1,128]{1,0:T(1,128)} %bitcast.15, bf16[128,128]{1,0:T(8,128)(2,1)} %weight_ref.2), custom_call_target="tpu_custom_call" | custom-call | flops 205520896 | bytes 8028160 | tf_op jit(solution)/shard_map/gate/pallas_call | solution.py:345
  75.3 21.6 %all-to-all-done.1 = bf16[128,56,128]{2,1,0:T(8,128)(2,1)} async-done(((bf16[128,56,128]{2,1,0:T(8,128)(2,1)}), bf16[128,56,128]{2,1,0:T(8,128)(2,1)}, u32[]{:S(2)}, u32[]{:S(2)}) %all-to-all-start.1) | async-done | bytes 1835040 | tf_op jit(solution)/shard_map/all_to_all | solution.py:381
  96.8 0.0 copy-done
  96.8 0.0 copy-done.1
  96.8 4.8 %finish.1 = bf16[112,7,8,128]{3,2,1,0:T(8,128)(2,1)} custom-call(bf16[128,7,8,128]{3,2,1,0:T(8,128)(2,1)} %bitcast.6.hidden_hbm, f32[112,7,8,128]{3,2,1,0:T(8,128)S(1)} %gate.1.gate_hbm, f32[1,128]{1,0:T(1,128)S(1)} %bitcast.9, bf16[128,128]{1,0:T(8,128)(2,1)S(1)} %copy-done), custom_call_target="tpu_custom_call" | custom-call | tf_op jit(solution)/shard_map/finish/pallas_call | solution.py:386
Async XLA Ops:
  63.7 33.1 %all-to-all-start.1 = ((bf16[128,56,128]{2,1,0:T(8,128)(2,1)}), bf16[128,56,128]{2,1,0:T(8,128)(2,1)}, u32[]{:S(2)}, u32[]{:S(2)}) async-start(bf16[128,56,128]{2,1,0:T(8,128)(2,1)} %bitcast.5), calls=%async_computation.1 | async-start | bytes 3670016 | tf_op jit(solution)/shard_map/all_to_all | solution.py:381
  69.2 27.6 %copy-start = (bf16[128,128]{1,0:T(8,128)(2,1)S(1)}, bf16[128,128]{1,0:T(8,128)(2,1)}, u32[]{:S(2)}) copy-start(bf16[128,128]{1,0:T(8,128)(2,1)} %weight_ref.3) | copy-start | bytes 98308
  69.3 27.6 %copy-start.1 = (f32[128]{0:T(128)S(1)}, f32[128]{0:T(128)}, u32[]{:S(2)}) copy-start(f32[128]{0:T(128)} %param.18) | copy-start | bytes 1540

commit v4 on v3

--- a/solution.py
+++ b/solution.py
@@ -18,13 +18,16 @@
 
 def project_kernel(
     pair_hbm,
-    mask_ref,
-    gain_ref,
-    left_gate_ref,
-    left_proj_ref,
-    right_gate_ref,
-    right_proj_ref,
+    mask_hbm,
+    gain_hbm,
+    left_gate_hbm,
+    left_proj_hbm,
+    right_gate_hbm,
+    right_proj_hbm,
     message_ref,
+    mask_in,
+    gain_in,
+    weights_in,
     pair_scr,
     weight_scr,
     center_scr,
@@ -37,9 +40,10 @@
     lower_b,
     spill_scr,
     sems,
+    small_sems,
 ):
     tile = pair_hbm.shape[0]
-    part = left_gate_ref.shape[0]
+    part = left_gate_hbm.shape[0]
     count = tile // chunk
     order = (count - 1, count - 2) + tuple(range(count - 2))
     normed_refs, uppers, lowers = (normed_a, normed_b), (upper_a, upper_b), (lower_a, lower_b)
@@ -48,19 +52,32 @@
         rows = pl.ds(c * chunk, chunk)
         return pltpu.make_async_copy(pair_hbm.at[rows], pair_scr.at[rows], sems.at[c])
 
-    for c in order:
+    sources = (left_gate_hbm, left_proj_hbm, right_gate_hbm, right_proj_hbm)
+    small = [
+        pltpu.make_async_copy(source, weights_in.at[place], small_sems.at[place])
+        for place, source in enumerate(sources)
+    ]
+    small.append(pltpu.make_async_copy(gain_hbm, gain_in, small_sems.at[4]))
+    small.append(pltpu.make_async_copy(mask_hbm, mask_in, small_sems.at[5]))
+    fetch(order[0]).start()
+    for copy in small:
+        copy.start()
+    for c in order[1:]:
         fetch(c).start()
-    gain = gain_ref[...] * 0.5
-    for place, ref in enumerate((left_gate_ref, left_proj_ref, right_gate_ref, right_proj_ref)):
-        weight_scr[place * part : (place + 1) * part, :] = (ref[...].astype(f32) * gain).astype(bf16)
     rows = lax.broadcasted_iota(jnp.int32, (lanes, lanes), 0)
     cols = lax.broadcasted_iota(jnp.int32, (lanes, lanes), 1)
     center_scr[...] = (jnp.where(rows == cols, 1.0, 0.0) - 1.0 / lanes).astype(bf16)
-    mask = mask_ref[...].astype(f32)
-    mask_scr[...] = jnp.concatenate([mask, mask[:, edge:]], axis=1)
     lane = lax.broadcasted_iota(jnp.int32, (1, lanes), 1)
     middle = (lane >= edge) & (lane < tile)
     spill_scr[:, 9 * 8 :, :] = jnp.zeros((part, 8, lanes), f32)
+    for copy in small:
+        copy.wait()
+    gain = gain_in[...] * 0.5
+    for place in range(4):
+        scaled = weights_in[place].astype(f32) * gain
+        weight_scr[place * part : (place + 1) * part, :] = scaled.astype(bf16)
+    mask = mask_in[...].astype(f32)
+    mask_scr[...] = jnp.concatenate([mask, mask[:, edge:]], axis=1)
 
     def norm(c, k, normed_ref):
         first, second = pair_scr[c * chunk + k], pair_scr[c * chunk + k + 1]
@@ -213,6 +230,8 @@
     turn_b,
     part_a,
     part_b,
+    center_scr,
+    scale_scr,
     hidden_sems,
     gate_sems,
     out_sems,
@@ -246,24 +265,26 @@
         return terms[0]
 
     def norm(g):
-        def block(c):
-            return hidden_scr[g, c : c + step].astype(f32)
-
-        starts = range(0, channels, step)
-        center = tree([jnp.sum(block(c), axis=0) for c in starts]) * (1.0 / channels)
-        squares = []
-        for c in starts:
-            centered = block(c) - center[None]
-            squares.append(jnp.sum(centered * centered, axis=0))
-        scale = lax.rsqrt(tree(squares) * (1.0 / channels) + epsilon)
-        for c in starts:
-            normed = (block(c) - center[None]) * scale[None]
-            turns[g % 2][c * 8 : (c + step) * 8] = normed.reshape(step * 8, lanes)
+        first = hidden_scr[g, 0].astype(f32)
+        sums, squares = [], []
+        for c in range(0, channels, step):
+            moved = hidden_scr[g, c : c + step].astype(f32) - first[None]
+            turns[g % 2][c * 8 : (c + step) * 8] = moved.reshape(step * 8, lanes)
+            sums.append(jnp.sum(moved, axis=0))
+            squares.append(jnp.sum(moved * moved, axis=0))
+        center = tree(sums) * (1.0 / channels)
+        spread = tree(squares) * (1.0 / channels) - center * center
+        center_scr[g % 2] = center
+        scale_scr[g % 2] = lax.rsqrt(jnp.maximum(spread, 0.0) + epsilon)
 
     def project(g, j):
-        row = turns[g % 2][pl.ds(j, channels, stride=8), :].astype(bf16)
+        moved = turns[g % 2][pl.ds(j, channels, stride=8), :]
+        center, scale = center_scr[g % 2, j : j + 1], scale_scr[g % 2, j : j + 1]
         projected = lax.dot_general(
-            row, weight_scr[...], (((0,), (0,)), ((), ())), preferred_element_type=f32
+            ((moved - center) * scale).astype(bf16),
+            weight_scr[...],
+            (((0,), (0,)), ((), ())),
+            preferred_element_type=f32,
         )
         outs[g % 2][pl.ds(j, edge, stride=8), :] = projected[:edge]
         outs[g % 2][pl.ds(edge * 8 + j, tile - edge, stride=8), :] = projected[tile:]
@@ -321,10 +342,13 @@
     turn_shape = pltpu.VMEM((2, part * 8, lanes), f32)
     message = pl.pallas_call(
         project_kernel,
-        in_specs=[anywhere] + [vmem] * 6,
+        in_specs=[anywhere] * 7,
         out_specs=vmem,
         out_shape=jax.ShapeDtypeStruct((part, 2 * tile - spill, lanes), bf16),
         scratch_shapes=[
+            pltpu.VMEM(pair_mask.shape, jnp.int32),
+            pltpu.VMEM((1, channels), f32),
+            pltpu.VMEM((4, part, channels), bf16),
             pltpu.VMEM(pair.shape, bf16),
             pltpu.VMEM((4 * part, channels), bf16),
             pltpu.VMEM((channels, channels), bf16),
@@ -337,6 +361,7 @@
             turn_shape,
             pltpu.VMEM((part, 80, lanes), f32),
             pltpu.SemaphoreType.DMA((tile // chunk,)),
+            pltpu.SemaphoreType.DMA((6,)),
         ],
         compiler_params=limit,
         name="project",
@@ -397,6 +422,8 @@
             pltpu.VMEM((channels * 8, lanes), f32),
             pltpu.VMEM((tile * 8, lanes), f32),
             pltpu.VMEM((tile * 8, lanes), f32),
+            pltpu.VMEM((2, 8, lanes), f32),
+            pltpu.VMEM((2, 8, lanes), f32),
             pltpu.SemaphoreType.DMA((groups,)),
             pltpu.SemaphoreType.DMA((groups,)),
             pltpu.SemaphoreType.DMA((groups,)),

time: 102 us -> 102 us (level)
  no operation moved by 1% of the time
where the time goes in v4:
time: 102 us; the launch traced here: 101 us
  blocking collectives  52.8 us (52%)
  waiting for transfers between devices  21.6 us (21%)
  Pallas kernels  21.3 us (21%)
  starting transfers between devices  5.45 us (5%)
    all_to_all x1, blocking collectives, shards(): received = lax.all_to_all(message, ('row', 'col'), 0, 0, tiled=True)  52.8 us
    all_to_all x1, waiting for transfers between devices, shards(): lax.all_to_all(hidden.reshape(rows * cols * ch, half, lanes), ('row', 'co...  21.6 us
    pallas_call x1, Pallas kernels, shards(): pl.pallas_call(project_kernel, in_specs=[anywhere] * 7, out_specs=vmem, o...  6.94 us
    pallas_call x1, Pallas kernels, shards(): pl.pallas_call(gate_kernel, grid=(tile // chunk,), in_specs=[pl.BlockSpec...  5.98 us
    all_to_all x1, starting transfers between devices, shards(): lax.all_to_all(hidden.reshape(rows * cols * ch, half, lanes), ('row', 'co...  5.45 us
    pallas_call x1, Pallas kernels, shards(): pl.pallas_call(finish_kernel, in_specs=[anywhere, anywhere, vmem, vmem],...  4.42 us
    pallas_call x1, Pallas kernels, shards(): pl.pallas_call(product_kernel, in_specs=[vmem], out_specs=anywhere, out_s...  3.95 us
  transfers between devices with their start and end apart: 1, of which 1 were waited for; matrix products, arithmetic and copies ran while one was open for 0% of the time, Pallas kernels for 6%

profile of v4, /device:TPU:1, one launch (start us, length us, event | category | flops | bytes accessed | tf_op | source)
XLA Modules:
  0.0 101.2 jit_solution(970653661083448305)
XLA Ops:
  0.0 6.9 %project.1 = bf16[64,200,128]{2,1,0:T(8,128)(2,1)S(1)} custom-call(bf16[112,112,128]{2,1,0:T(8,128)(2,1)} %pair_ref.1, s32[112,112]{1,0:T(8,128)} %mask_hbm.1, f32[1,128]{1,0:T(1,128)} %bitcast.14, bf16[64,128]{1,0:T(8,128)(2,1)} %bitcast.10, bf16[64,128]{1,0:T(8,128)(2,1)} %bitcast.11, bf16[64,128]{1,0:T(8,128)(2,1)} %bitcast.12, bf16[64,128]{1,0:T(8,128)(2,1)} %bitcast.13), custom_call_target="tpu_custom_call" | custom-call | tf_op jit(solution)/shard_map/project/pallas_call | solution.py:343
  7.0 52.8 %all_to_all.10.received_ref = bf16[64,200,128]{2,1,0:T(8,128)(2,1)S(1)} all-to-all(bf16[64,200,128]{2,1,0:T(8,128)(2,1)S(1)} %project.1), channel_id=1, replica_groups=mesh['row'=8,'col'=8,'ch'=2] {'row','col'}, dimensions={0} | all-to-all | bytes 6553600 | tf_op jit(solution)/shard_map/all_to_all | solution.py:389
  59.8 3.9 %product.1 = bf16[8,896,128]{2,1,0:T(8,128)(2,1)} custom-call(bf16[64,200,128]{2,1,0:T(8,128)(2,1)S(1)} %all_to_all.10.received_ref), custom_call_target="tpu_custom_call" | custom-call | tf_op jit(solution)/shard_map/product/pallas_call | solution.py:391
  63.7 5.4 %all-to-all-start.1 = ((bf16[128,56,128]{2,1,0:T(8,128)(2,1)}), bf16[128,56,128]{2,1,0:T(8,128)(2,1)}, u32[]{:S(2)}, u32[]{:S(2)}) async-start(bf16[128,56,128]{2,1,0:T(8,128)(2,1)} %bitcast.5), calls=%async_computation.1 | async-start | bytes 3670016 | tf_op jit(solution)/shard_map/all_to_all | solution.py:406
  69.2 0.0 copy-start
  69.2 0.0 copy-start.1
  69.2 6.0 %gate.1.gate_hbm = f32[112,7,8,128]{3,2,1,0:T(8,128)S(1)} custom-call(bf16[112,112,128]{2,1,0:T(8,128)(2,1)} %pair_ref.1, f32[1,128]{1,0:T(1,128)} %bitcast.15, bf16[128,128]{1,0:T(8,128)(2,1)} %weight_ref.2), custom_call_target="tpu_custom_call" | custom-call | flops 205520896 | bytes 8028160 | tf_op jit(solution)/shard_map/gate/pallas_call | solution.py:370
  75.2 21.6 %all-to-all-done.1 = bf16[128,56,128]{2,1,0:T(8,128)(2,1)} async-done(((bf16[128,56,128]{2,1,0:T(8,128)(2,1)}), bf16[128,56,128]{2,1,0:T(8,128)(2,1)}, u32[]{:S(2)}, u32[]{:S(2)}) %all-to-all-start.1) | async-done | bytes 1835040 | tf_op jit(solution)/shard_map/all_to_all | solution.py:406
  96.7 0.0 copy-done
  96.7 0.0 copy-done.1
  96.8 4.4 %finish.1 = bf16[112,7,8,128]{3,2,1,0:T(8,128)(2,1)} custom-call(bf16[128,7,8,128]{3,2,1,0:T(8,128)(2,1)} %bitcast.6.hidden_hbm, f32[112,7,8,128]{3,2,1,0:T(8,128)S(1)} %gate.1.gate_hbm, f32[1,128]{1,0:T(1,128)S(1)} %bitcast.9, bf16[128,128]{1,0:T(8,128)(2,1)S(1)} %copy-done), custom_call_target="tpu_custom_call" | custom-call | tf_op jit(solution)/shard_map/finish/pallas_call | solution.py:411
Async XLA Ops:
  63.7 33.0 %all-to-all-start.1 = ((bf16[128,56,128]{2,1,0:T(8,128)(2,1)}), bf16[128,56,128]{2,1,0:T(8,128)(2,1)}, u32[]{:S(2)}, u32[]{:S(2)}) async-start(bf16[128,56,128]{2,1,0:T(8,128)(2,1)} %bitcast.5), calls=%async_computation.1 | async-start | bytes 3670016 | tf_op jit(solution)/shard_map/all_to_all | solution.py:406
  69.2 27.6 %copy-start = (bf16[128,128]{1,0:T(8,128)(2,1)S(1)}, bf16[128,128]{1,0:T(8,128)(2,1)}, u32[]{:S(2)}) copy-start(bf16[128,128]{1,0:T(8,128)(2,1)} %weight_ref.3) | copy-start | bytes 98308
  69.2 27.6 %copy-start.1 = (f32[128]{0:T(128)S(1)}, f32[128]{0:T(128)}, u32[]{:S(2)}) copy-start(f32[128]{0:T(128)} %param.18) | copy-start | bytes 1540

commit v5 on v4

--- a/solution.py
+++ b/solution.py
@@ -62,8 +62,7 @@
     fetch(order[0]).start()
     for copy in small:
         copy.start()
-    for c in order[1:]:
-        fetch(c).start()
+    fetch(order[1]).start()
     rows = lax.broadcasted_iota(jnp.int32, (lanes, lanes), 0)
     cols = lax.broadcasted_iota(jnp.int32, (lanes, lanes), 1)
     center_scr[...] = (jnp.where(rows == cols, 1.0, 0.0) - 1.0 / lanes).astype(bf16)
@@ -131,6 +130,8 @@
     for step in range(count + 2):
         if step < count:
             fetch(order[step]).wait()
+            if step + 2 < count:
+                fetch(order[step + 2]).start()
         for k in range(0, chunk, 2):
             if step < count:
                 norm(order[step], k, normed_refs[step % 2])
@@ -160,10 +161,11 @@
     gate_ref[...] = sigmoid(gate).reshape(gate_ref.shape)
 
 
-def product_kernel(received_ref, out_hbm, right_a, right_b, out_scr, sems):
-    rows, half_cols, tile = 8, 4, received_ref.shape[1] - 88
-    cols, steps = 2 * half_cols, rows // 2
-    rights = (right_a, right_b)
+def product_kernel(received_ref, out_hbm, right_a, right_b, right_c, right_d, out_scr, sems):
+    rows, cols, tile = 8, 8, out_hbm.shape[1] // 8
+    rights = (right_a, right_b, right_c, right_d)
+    blocks_count, steps = len(rights), out_scr.shape[0]
+    share, wide = cols // blocks_count, rows // steps
     lane = lax.broadcasted_iota(jnp.int32, (1, lanes), 1)
 
     def turn(q):
@@ -183,36 +185,40 @@
                 parts.append(jnp.where(lane < 32, pieces[0], eight))
             blocks.append(jnp.concatenate(parts, axis=0).astype(bf16))
         block = jnp.concatenate(blocks, axis=0)
-        at = (q % half_cols) * tile
-        rights[q // half_cols][at : at + tile, :] = block.T[:tile]
+        at = (q % share) * tile
+        rights[q // share][at : at + tile, :] = block.T[:tile]
 
     def send(s, h):
-        width = half_cols * tile
+        width = share * tile
         return pltpu.make_async_copy(
-            out_scr.at[s, h], out_hbm.at[pl.ds(2 * s, 2), pl.ds(h * width, width)], sems.at[s, h]
+            out_scr.at[s, h],
+            out_hbm.at[pl.ds(wide * s, wide), pl.ds(h * width, width)],
+            sems.at[s, h],
         )
 
     def multiply(s, h):
         lefts = [
-            jnp.concatenate([received_ref[r * cols + 2 * s + p, :tile] for r in range(rows)], axis=0)
-            for p in range(2)
+            jnp.concatenate(
+                [received_ref[r * cols + wide * s + p, :tile] for r in range(rows)], axis=0
+            )
+            for p in range(wide)
         ]
         hidden = jnp.dot(
             rights[h][...], jnp.concatenate(lefts, axis=1), preferred_element_type=f32
         ).astype(bf16)
-        for p in range(2):
+        for p in range(wide):
             out_scr[s, h, p] = hidden[:, p * lanes : (p + 1) * lanes]
         send(s, h).start()
 
-    for q in range(half_cols):
+    for q in range(share):
         turn(q)
-    for s in range(steps):
-        turn(half_cols + s)
-        multiply(s, 0)
-    for s in range(steps):
-        multiply(s, 1)
-    for s in range(steps):
-        for h in range(2):
+    for h in range(blocks_count):
+        for s in range(steps):
+            if h + 1 < blocks_count:
+                turn((h + 1) * share + s)
+            multiply(s, h)
+    for h in range(blocks_count):
+        for s in range(steps):
             send(s, h).wait()
 
 
@@ -388,16 +394,19 @@
 
     received = lax.all_to_all(message, ("row", "col"), 0, 0, tiled=True)
 
+    right_shape = pltpu.VMEM((cols * tile // 4, rows * tile), bf16)
     hidden = pl.pallas_call(
         product_kernel,
         in_specs=[vmem],
         out_specs=anywhere,
         out_shape=jax.ShapeDtypeStruct((rows, cols * tile, lanes), bf16),
         scratch_shapes=[
-            pltpu.VMEM((cols * tile // 2, rows * tile), bf16),
-            pltpu.VMEM((cols * tile // 2, rows * tile), bf16),
-            pltpu.VMEM((rows // 2, 2, 2, cols * tile // 2, lanes), bf16),
-            pltpu.SemaphoreType.DMA((rows // 2, 2)),
+            right_shape,
+            right_shape,
+            right_shape,
+            right_shape,
+            pltpu.VMEM((2, 4, rows // 2, cols * tile // 4, lanes), bf16),
+            pltpu.SemaphoreType.DMA((2, 4)),
         ],
         compiler_params=limit,
         name="product",

time: 102 us -> 100 us (0.980)
  Pallas kernels: 21.3 us -> 20.1 us
where the time goes in v5:
time: 100 us
  blocking collectives  52.8 us (53%)
  waiting for transfers between devices  21.6 us (22%)
  Pallas kernels  20.1 us (20%)
  starting transfers between devices  5.45 us (5%)
    all_to_all x1, blocking collectives, shards(): received = lax.all_to_all(message, ('row', 'col'), 0, 0, tiled=True)  52.8 us
    all_to_all x1, waiting for transfers between devices, shards(): lax.all_to_all(hidden.reshape(rows * cols * ch, half, lanes), ('row', 'co...  21.6 us
    pallas_call x1, Pallas kernels, shards(): pl.pallas_call(project_kernel, in_specs=[anywhere] * 7, out_specs=vmem, o...  6.33 us
    pallas_call x1, Pallas kernels, shards(): pl.pallas_call(gate_kernel, grid=(tile // chunk,), in_specs=[pl.BlockSpec...  5.98 us
    all_to_all x1, starting transfers between devices, shards(): lax.all_to_all(hidden.reshape(rows * cols * ch, half, lanes), ('row', 'co...  5.45 us
    pallas_call x1, Pallas kernels, shards(): pl.pallas_call(finish_kernel, in_specs=[anywhere, anywhere, vmem, vmem],...  4.42 us
    pallas_call x1, Pallas kernels, shards(): pl.pallas_call(product_kernel, in_specs=[vmem], out_specs=anywhere, out_s...  3.36 us
  transfers between devices with their start and end apart: 1, of which 1 were waited for; matrix products, arithmetic and copies ran while one was open for 0% of the time, Pallas kernels for 6%

profile of v5, /device:TPU:1, one launch (start us, length us, event | category | flops | bytes accessed | tf_op | source)
XLA Modules:
  0.0 100.0 jit_solution(16146545177748608082)
XLA Ops:
  0.0 6.3 %project.1 = bf16[64,200,128]{2,1,0:T(8,128)(2,1)S(1)} custom-call(bf16[112,112,128]{2,1,0:T(8,128)(2,1)} %pair_ref.1, s32[112,112]{1,0:T(8,128)} %mask_hbm.1, f32[1,128]{1,0:T(1,128)} %bitcast.14, bf16[64,128]{1,0:T(8,128)(2,1)} %bitcast.10, bf16[64,128]{1,0:T(8,128)(2,1)} %bitcast.11, bf16[64,128]{1,0:T(8,128)(2,1)} %bitcast.12, bf16[64,128]{1,0:T(8,128)(2,1)} %bitcast.13), custom_call_target="tpu_custom_call" | custom-call | tf_op jit(solution)/shard_map/project/pallas_call | solution.py:349
  6.3 52.8 %all_to_all.10.received_ref = bf16[64,200,128]{2,1,0:T(8,128)(2,1)S(1)} all-to-all(bf16[64,200,128]{2,1,0:T(8,128)(2,1)S(1)} %project.1), channel_id=1, replica_groups=mesh['row'=8,'col'=8,'ch'=2] {'row','col'}, dimensions={0} | all-to-all | bytes 6553600 | tf_op jit(solution)/shard_map/all_to_all | solution.py:395
  59.1 3.4 %product.1 = bf16[8,896,128]{2,1,0:T(8,128)(2,1)} custom-call(bf16[64,200,128]{2,1,0:T(8,128)(2,1)S(1)} %all_to_all.10.received_ref), custom_call_target="tpu_custom_call" | custom-call | tf_op jit(solution)/shard_map/product/pallas_call | solution.py:398
  62.5 5.4 %all-to-all-start.1 = ((bf16[128,56,128]{2,1,0:T(8,128)(2,1)}), bf16[128,56,128]{2,1,0:T(8,128)(2,1)}, u32[]{:S(2)}, u32[]{:S(2)}) async-start(bf16[128,56,128]{2,1,0:T(8,128)(2,1)} %bitcast.5), calls=%async_computation.1 | async-start | bytes 3670016 | tf_op jit(solution)/shard_map/all_to_all | solution.py:415
  68.0 0.0 copy-start
  68.0 0.0 copy-start.1
  68.0 6.0 %gate.1.gate_hbm = f32[112,7,8,128]{3,2,1,0:T(8,128)S(1)} custom-call(bf16[112,112,128]{2,1,0:T(8,128)(2,1)} %pair_ref.1, f32[1,128]{1,0:T(1,128)} %bitcast.15, bf16[128,128]{1,0:T(8,128)(2,1)} %weight_ref.2), custom_call_target="tpu_custom_call" | custom-call | flops 205520896 | bytes 8028160 | tf_op jit(solution)/shard_map/gate/pallas_call | solution.py:376
  74.0 21.6 %all-to-all-done.1 = bf16[128,56,128]{2,1,0:T(8,128)(2,1)} async-done(((bf16[128,56,128]{2,1,0:T(8,128)(2,1)}), bf16[128,56,128]{2,1,0:T(8,128)(2,1)}, u32[]{:S(2)}, u32[]{:S(2)}) %all-to-all-start.1) | async-done | bytes 1835040 | tf_op jit(solution)/shard_map/all_to_all | solution.py:415
  95.5 0.0 copy-done
  95.5 0.0 copy-done.1
  95.6 4.4 %finish.1 = bf16[112,7,8,128]{3,2,1,0:T(8,128)(2,1)} custom-call(bf16[128,7,8,128]{3,2,1,0:T(8,128)(2,1)} %bitcast.6.hidden_hbm, f32[112,7,8,128]{3,2,1,0:T(8,128)S(1)} %gate.1.gate_hbm, f32[1,128]{1,0:T(1,128)S(1)} %bitcast.9, bf16[128,128]{1,0:T(8,128)(2,1)S(1)} %copy-done), custom_call_target="tpu_custom_call" | custom-call | tf_op jit(solution)/shard_map/finish/pallas_call | solution.py:420
Async XLA Ops:
  62.5 33.0 %all-to-all-start.1 = ((bf16[128,56,128]{2,1,0:T(8,128)(2,1)}), bf16[128,56,128]{2,1,0:T(8,128)(2,1)}, u32[]{:S(2)}, u32[]{:S(2)}) async-start(bf16[128,56,128]{2,1,0:T(8,128)(2,1)} %bitcast.5), calls=%async_computation.1 | async-start | bytes 3670016 | tf_op jit(solution)/shard_map/all_to_all | solution.py:415
  68.0 27.6 %copy-start = (bf16[128,128]{1,0:T(8,128)(2,1)S(1)}, bf16[128,128]{1,0:T(8,128)(2,1)}, u32[]{:S(2)}) copy-start(bf16[128,128]{1,0:T(8,128)(2,1)} %weight_ref.3) | copy-start | bytes 98308
  68.0 27.6 %copy-start.1 = (f32[128]{0:T(128)S(1)}, f32[128]{0:T(128)}, u32[]{:S(2)}) copy-start(f32[128]{0:T(128)} %param.18) | copy-start | bytes 1540

commit v6 on v5

--- a/solution.py
+++ b/solution.py
@@ -128,10 +128,15 @@
             message_ref[own, tile + at : tile + at + chunk, :] = rows.astype(bf16)
 
     for step in range(count + 2):
-        if step < count:
-            fetch(order[step]).wait()
-            if step + 2 < count:
-                fetch(order[step + 2]).start()
+        if step == 0:
+            fetch(order[0]).wait()
+            for c in order[2:]:
+                fetch(c).start()
+        if step == 1:
+            fetch(order[1]).wait()
+        if step == 2:
+            for c in order[2:]:
+                fetch(c).wait()
         for k in range(0, chunk, 2):
             if step < count:
                 norm(order[step], k, normed_refs[step % 2])
@@ -162,7 +167,8 @@
 
 
 def product_kernel(received_ref, out_hbm, right_a, right_b, right_c, right_d, out_scr, sems):
-    rows, cols, tile = 8, 8, out_hbm.shape[1] // 8
+    ch, rows, cols, groups = out_hbm.shape[:4]
+    tile = ch * groups * 8
     rights = (right_a, right_b, right_c, right_d)
     blocks_count, steps = len(rights), out_scr.shape[0]
     share, wide = cols // blocks_count, rows // steps
@@ -188,12 +194,11 @@
         at = (q % share) * tile
         rights[q // share][at : at + tile, :] = block.T[:tile]
 
-    def send(s, h):
-        width = share * tile
+    def send(s, h, side):
         return pltpu.make_async_copy(
-            out_scr.at[s, h],
-            out_hbm.at[pl.ds(wide * s, wide), pl.ds(h * width, width)],
-            sems.at[s, h],
+            out_scr.at[s, h, side],
+            out_hbm.at[side, pl.ds(wide * s, wide), pl.ds(share * h, share)],
+            sems.at[s, h, side],
         )
 
     def multiply(s, h):
@@ -205,10 +210,13 @@
         ]
         hidden = jnp.dot(
             rights[h][...], jnp.concatenate(lefts, axis=1), preferred_element_type=f32
-        ).astype(bf16)
+        )
         for p in range(wide):
-            out_scr[s, h, p] = hidden[:, p * lanes : (p + 1) * lanes]
-        send(s, h).start()
+            own = hidden[:, p * lanes : (p + 1) * lanes].reshape(share, ch, groups, 8, lanes)
+            for side in range(ch):
+                out_scr[s, h, side, p] = own[:, side].astype(bf16)
+        for side in range(ch):
+            send(s, h, side).start()
 
     for q in range(share):
         turn(q)
@@ -219,17 +227,17 @@
             multiply(s, h)
     for h in range(blocks_count):
         for s in range(steps):
-            send(s, h).wait()
+            for side in range(ch):
+                send(s, h, side).wait()
 
 
 def finish_kernel(
     hidden_hbm,
-    gate_hbm,
+    gate_ref,
     gain_ref,
     weight_ref,
     out_hbm,
     hidden_scr,
-    gate_scr,
     out_scr,
     weight_scr,
     turn_a,
@@ -239,7 +247,6 @@
     center_scr,
     scale_scr,
     hidden_sems,
-    gate_sems,
     out_sems,
 ):
     groups, channels, tile = hidden_scr.shape[0], hidden_scr.shape[1], out_scr.shape[1]
@@ -249,21 +256,13 @@
     def fetch_hidden(g):
         return pltpu.make_async_copy(hidden_hbm.at[:, g], hidden_scr.at[g], hidden_sems.at[g])
 
-    def fetch_gate(g):
-        return pltpu.make_async_copy(gate_hbm.at[:, g], gate_scr.at[g], gate_sems.at[g])
-
     def send(g):
         return pltpu.make_async_copy(out_scr.at[g], out_hbm.at[:, g], out_sems.at[g])
 
     for g in range(groups):
         fetch_hidden(g).start()
-    for g in range(groups):
-        fetch_gate(g).start()
     scaled = jnp.broadcast_to(gain_ref[...], (channels, channels)).T * weight_ref[...].astype(f32)
-    part = channels // 2
-    for side in range(2):
-        turn_a[pl.ds(side, part, stride=2), :] = scaled[side * part : (side + 1) * part]
-    weight_scr[...] = turn_a[:channels, :].astype(bf16)
+    weight_scr[...] = scaled.astype(bf16)
 
     def tree(terms):
         while len(terms) > 1:
@@ -299,13 +298,12 @@
         count = tile // 8
         own = slice(n * count, (n + 1) * count)
         rows = outs[g % 2][n * count * 8 : (n + 1) * count * 8].reshape(count, 8, lanes)
-        out_scr[g, own] = (rows * gate_scr[g, own]).astype(bf16)
-
+        out_scr[g, own] = (rows * gate_ref[own, g]).astype(bf16)
+
+    arrivals = {0: (0,), 1: (1, 2), 3: tuple(range(3, groups))}
     for s in range(groups + 2):
-        if s < groups:
-            fetch_hidden(s).wait()
-        if 2 <= s:
-            fetch_gate(s - 2).wait()
+        for g in arrivals.get(s, ()):
+            fetch_hidden(g).wait()
         if s < groups:
             norm(s)
         for j in range(8):
@@ -399,32 +397,30 @@
         product_kernel,
         in_specs=[vmem],
         out_specs=anywhere,
-        out_shape=jax.ShapeDtypeStruct((rows, cols * tile, lanes), bf16),
+        out_shape=jax.ShapeDtypeStruct((ch, rows, cols, groups, 8, lanes), bf16),
         scratch_shapes=[
             right_shape,
             right_shape,
             right_shape,
             right_shape,
-            pltpu.VMEM((2, 4, rows // 2, cols * tile // 4, lanes), bf16),
-            pltpu.SemaphoreType.DMA((2, 4)),
+            pltpu.VMEM((2, 4, ch, rows // 2, cols // 4, groups, 8, lanes), bf16),
+            pltpu.SemaphoreType.DMA((2, 4, ch)),
         ],
         compiler_params=limit,
         name="product",
     )(received)
 
     parts = lax.all_to_all(
-        hidden.reshape(rows * cols * ch, half, lanes), ("row", "col", "ch"), 0, 0, tiled=True
+        hidden.reshape(channels, groups, 8, lanes), ("ch", "row", "col"), 0, 0, tiled=True
     )
-    parts = parts.reshape(channels, groups, 8, lanes)
 
     update = pl.pallas_call(
         finish_kernel,
-        in_specs=[anywhere, anywhere, vmem, vmem],
+        in_specs=[anywhere, vmem, vmem, vmem],
         out_specs=anywhere,
         out_shape=jax.ShapeDtypeStruct((tile, groups, 8, lanes), bf16),
         scratch_shapes=[
             pltpu.VMEM((groups, channels, 8, lanes), bf16),
-            pltpu.VMEM((groups, tile, 8, lanes), f32),
             pltpu.VMEM((groups, tile, 8, lanes), bf16),
             pltpu.VMEM((channels, channels), bf16),
             pltpu.VMEM((channels * 8, lanes), f32),
@@ -433,7 +429,6 @@
             pltpu.VMEM((tile * 8, lanes), f32),
             pltpu.VMEM((2, 8, lanes), f32),
             pltpu.VMEM((2, 8, lanes), f32),
-            pltpu.SemaphoreType.DMA((groups,)),
             pltpu.SemaphoreType.DMA((groups,)),
             pltpu.SemaphoreType.DMA((groups,)),
         ],

time: 100 us -> 98.8 us (0.988)
  waiting for transfers between devices: 21.6 us -> 20.1 us
    all_to_all x1, waiting for transfers between devices: 21.6 us -> 20.1 us  [shards(): lax.all_to_all(hidden.reshape(channels, groups, 8, lanes), ('ch', 'row',...]
where the time goes in v6:
time: 98.8 us; the launch traced here: 98.1 us
  blocking collectives  52.8 us (53%)
  waiting for transfers between devices  20.1 us (20%)
  Pallas kernels  19.7 us (20%)
  starting transfers between devices  5.47 us (6%)
    all_to_all x1, blocking collectives, shards(): received = lax.all_to_all(message, ('row', 'col'), 0, 0, tiled=True)  52.8 us
    all_to_all x1, waiting for transfers between devices, shards(): lax.all_to_all(hidden.reshape(channels, groups, 8, lanes), ('ch', 'row',...  20.1 us
    pallas_call x1, Pallas kernels, shards(): pl.pallas_call(project_kernel, in_specs=[anywhere] * 7, out_specs=vmem, o...  6.12 us
    pallas_call x1, Pallas kernels, shards(): pl.pallas_call(gate_kernel, grid=(tile // chunk,), in_specs=[pl.BlockSpec...  5.98 us
    all_to_all x1, starting transfers between devices, shards(): lax.all_to_all(hidden.reshape(channels, groups, 8, lanes), ('ch', 'row',...  5.47 us
    pallas_call x1, Pallas kernels, shards(): pl.pallas_call(finish_kernel, in_specs=[anywhere, vmem, vmem, vmem], out_...  4.1 us
    pallas_call x1, Pallas kernels, shards(): pl.pallas_call(product_kernel, in_specs=[vmem], out_specs=anywhere, out_s...  3.46 us
  transfers between devices with their start and end apart: 1, of which 1 were waited for; matrix products, arithmetic and copies ran while one was open for 0% of the time, Pallas kernels for 6%

profile of v6, /device:TPU:1, one launch (start us, length us, event | category | flops | bytes accessed | tf_op | source)
XLA Modules:
  0.0 98.1 jit_solution(16087481446440458838)
XLA Ops:
  0.0 6.1 %project.1 = bf16[64,200,128]{2,1,0:T(8,128)(2,1)S(1)} custom-call(bf16[112,112,128]{2,1,0:T(8,128)(2,1)} %pair_ref.1, s32[112,112]{1,0:T(8,128)} %mask_hbm.1, f32[1,128]{1,0:T(1,128)} %bitcast.13, bf16[64,128]{1,0:T(8,128)(2,1)} %bitcast.9, bf16[64,128]{1,0:T(8,128)(2,1)} %bitcast.10, bf16[64,128]{1,0:T(8,128)(2,1)} %bitcast.11, bf16[64,128]{1,0:T(8,128)(2,1)} %bitcast.12), custom_call_target="tpu_custom_call" | custom-call | tf_op jit(solution)/shard_map/project/pallas_call | solution.py:347
  6.1 52.8 %all_to_all.10.received_ref = bf16[64,200,128]{2,1,0:T(8,128)(2,1)S(1)} all-to-all(bf16[64,200,128]{2,1,0:T(8,128)(2,1)S(1)} %project.1), channel_id=1, replica_groups=mesh['row'=8,'col'=8,'ch'=2] {'row','col'}, dimensions={0} | all-to-all | bytes 6553600 | tf_op jit(solution)/shard_map/all_to_all | solution.py:393
  58.9 3.5 %product.1 = bf16[2,8,8,7,8,128]{5,4,3,2,1,0:T(8,128)(2,1)} custom-call(bf16[64,200,128]{2,1,0:T(8,128)(2,1)S(1)} %all_to_all.10.received_ref), custom_call_target="tpu_custom_call" | custom-call | tf_op jit(solution)/shard_map/product/pallas_call | solution.py:396
  62.4 5.5 %all-to-all-start.1 = ((bf16[128,7,8,128]{3,2,1,0:T(8,128)(2,1)}), bf16[128,7,8,128]{3,2,1,0:T(8,128)(2,1)}, u32[]{:S(2)}, u32[]{:S(2)}) async-start(bf16[128,7,8,128]{3,2,1,0:T(8,128)(2,1)} %bitcast.5), calls=%async_computation.1 | async-start | bytes 3670016 | tf_op jit(solution)/shard_map/all_to_all | solution.py:413
  67.9 0.0 copy-start
  67.9 0.0 copy-start.1
  67.9 6.0 %gate.1.gate_ref = f32[112,7,8,128]{3,2,1,0:T(8,128)S(1)} custom-call(bf16[112,112,128]{2,1,0:T(8,128)(2,1)} %pair_ref.1, f32[1,128]{1,0:T(1,128)} %bitcast.14, bf16[128,128]{1,0:T(8,128)(2,1)} %weight_ref.2), custom_call_target="tpu_custom_call" | custom-call | flops 205520896 | bytes 8028160 | tf_op jit(solution)/shard_map/gate/pallas_call | solution.py:374
  73.9 20.1 %all-to-all-done.1.hidden_hbm = bf16[128,7,8,128]{3,2,1,0:T(8,128)(2,1)} async-done(((bf16[128,7,8,128]{3,2,1,0:T(8,128)(2,1)}), bf16[128,7,8,128]{3,2,1,0:T(8,128)(2,1)}, u32[]{:S(2)}, u32[]{:S(2)}) %all-to-all-start.1) | async-done | bytes 1835040 | tf_op jit(solution)/shard_map/all_to_all | solution.py:413
  94.0 0.0 copy-done
  94.0 0.0 copy-done.1
  94.0 4.1 %finish.1 = bf16[112,7,8,128]{3,2,1,0:T(8,128)(2,1)} custom-call(bf16[128,7,8,128]{3,2,1,0:T(8,128)(2,1)} %all-to-all-done.1.hidden_hbm, f32[112,7,8,128]{3,2,1,0:T(8,128)S(1)} %gate.1.gate_ref, f32[1,128]{1,0:T(1,128)S(1)} %bitcast.8, bf16[128,128]{1,0:T(8,128)(2,1)S(1)} %copy-done), custom_call_target="tpu_custom_call" | custom-call | tf_op jit(solution)/shard_map/finish/pallas_call | solution.py:417
Async XLA Ops:
  62.4 31.6 %all-to-all-start.1 = ((bf16[128,7,8,128]{3,2,1,0:T(8,128)(2,1)}), bf16[128,7,8,128]{3,2,1,0:T(8,128)(2,1)}, u32[]{:S(2)}, u32[]{:S(2)}) async-start(bf16[128,7,8,128]{3,2,1,0:T(8,128)(2,1)} %bitcast.5), calls=%async_computation.1 | async-start | bytes 3670016 | tf_op jit(solution)/shard_map/all_to_all | solution.py:413
  67.9 26.1 %copy-start = (bf16[128,128]{1,0:T(8,128)(2,1)S(1)}, bf16[128,128]{1,0:T(8,128)(2,1)}, u32[]{:S(2)}) copy-start(bf16[128,128]{1,0:T(8,128)(2,1)} %weight_ref.3) | copy-start | bytes 98308
  67.9 26.1 %copy-start.1 = (f32[128]{0:T(128)S(1)}, f32[128]{0:T(128)}, u32[]{:S(2)}) copy-start(f32[128]{0:T(128)} %param.18) | copy-start | bytes 1540

commit v7 on v6

--- a/solution.py
+++ b/solution.py
@@ -83,18 +83,19 @@
         source = jnp.concatenate([first, first[edge:], second, second[edge:]], axis=0)
         centered = lax.dot_general(center_scr[...], source, turned, preferred_element_type=f32)
         spread = jnp.sum(centered * centered, axis=0, keepdims=True) * (1.0 / lanes)
-        normed_ref[k // 2] = (centered * lax.rsqrt(spread + epsilon)).astype(bf16)
-
-    def values(c, k, normed_ref, upper, lower):
+        at = c * chunk + k
+        valid = jnp.concatenate([mask_scr[at : at + 1, :], mask_scr[at + 1 : at + 2, :]], axis=1)
+        normed_ref[k // 2] = (centered * (lax.rsqrt(spread + epsilon) * valid)).astype(bf16)
+
+    def values(k, normed_ref, upper, lower):
         normed = normed_ref[k // 2]
         left = jnp.dot(weight_scr[: 2 * part], normed, preferred_element_type=f32)
         right = jnp.dot(weight_scr[2 * part :], normed, preferred_element_type=f32)
         for kk in range(2):
             own = slice(kk * lanes, (kk + 1) * lanes)
             row = k + kk
-            valid = mask_scr[c * chunk + row : c * chunk + row + 1, :]
-            left_vals = (jnp.tanh(left[:part, own]) + 1.0) * left[part:, own] * valid
-            right_vals = (jnp.tanh(right[:part, own]) + 1.0) * right[part:, own] * valid
+            left_vals = (jnp.tanh(left[:part, own]) + 1.0) * left[part:, own]
+            right_vals = (jnp.tanh(right[:part, own]) + 1.0) * right[part:, own]
             place = pl.ds(row % 8, part, stride=8)
             upper[row // 8, place, :] = jnp.where(middle, right_vals, left_vals)
             lower[row // 8, place, :] = right_vals
@@ -142,7 +143,7 @@
                 norm(order[step], k, normed_refs[step % 2])
             if 1 <= step < count + 1:
                 last = (step - 1) % 2
-                values(order[step - 1], k, normed_refs[last], uppers[last], lowers[last])
+                values(k, normed_refs[last], uppers[last], lowers[last])
             if 2 <= step:
                 store(order[step - 2], k * part // chunk, uppers[step % 2], lowers[step % 2])
 

time: 98.8 us -> 98.7 us (level)
  no operation moved by 1% of the time
where the time goes in v7:
time: 98.7 us; the launch traced here: 98 us
  blocking collectives  52.8 us (53%)
  waiting for transfers between devices  20.1 us (20%)
  Pallas kernels  19.5 us (20%)
  starting transfers between devices  5.46 us (6%)
    all_to_all x1, blocking collectives, shards(): received = lax.all_to_all(message, ('row', 'col'), 0, 0, tiled=True)  52.8 us
    all_to_all x1, waiting for transfers between devices, shards(): lax.all_to_all(hidden.reshape(channels, groups, 8, lanes), ('ch', 'row',...  20.1 us
    pallas_call x1, Pallas kernels, shards(): pl.pallas_call(project_kernel, in_specs=[anywhere] * 7, out_specs=vmem, o...  5.99 us
    pallas_call x1, Pallas kernels, shards(): pl.pallas_call(gate_kernel, grid=(tile // chunk,), in_specs=[pl.BlockSpec...  5.98 us
    all_to_all x1, starting transfers between devices, shards(): lax.all_to_all(hidden.reshape(channels, groups, 8, lanes), ('ch', 'row',...  5.46 us
    pallas_call x1, Pallas kernels, shards(): pl.pallas_call(finish_kernel, in_specs=[anywhere, vmem, vmem, vmem], out_...  4.1 us
    pallas_call x1, Pallas kernels, shards(): pl.pallas_call(product_kernel, in_specs=[vmem], out_specs=anywhere, out_s...  3.46 us
  transfers between devices with their start and end apart: 1, of which 1 were waited for; matrix products, arithmetic and copies ran while one was open for 0% of the time, Pallas kernels for 6%

profile of v7, /device:TPU:1, one launch (start us, length us, event | category | flops | bytes accessed | tf_op | source)
XLA Modules:
  0.0 98.0 jit_solution(17944113286028724457)
XLA Ops:
  0.0 6.0 %project.1 = bf16[64,200,128]{2,1,0:T(8,128)(2,1)S(1)} custom-call(bf16[112,112,128]{2,1,0:T(8,128)(2,1)} %pair_ref.1, s32[112,112]{1,0:T(8,128)} %mask_hbm.1, f32[1,128]{1,0:T(1,128)} %bitcast.13, bf16[64,128]{1,0:T(8,128)(2,1)} %bitcast.9, bf16[64,128]{1,0:T(8,128)(2,1)} %bitcast.10, bf16[64,128]{1,0:T(8,128)(2,1)} %bitcast.11, bf16[64,128]{1,0:T(8,128)(2,1)} %bitcast.12), custom_call_target="tpu_custom_call" | custom-call | tf_op jit(solution)/shard_map/project/pallas_call | solution.py:348
  6.0 52.8 %all_to_all.10.received_ref = bf16[64,200,128]{2,1,0:T(8,128)(2,1)S(1)} all-to-all(bf16[64,200,128]{2,1,0:T(8,128)(2,1)S(1)} %project.1), channel_id=1, replica_groups=mesh['row'=8,'col'=8,'ch'=2] {'row','col'}, dimensions={0} | all-to-all | bytes 6553600 | tf_op jit(solution)/shard_map/all_to_all | solution.py:394
  58.8 3.5 %product.1 = bf16[2,8,8,7,8,128]{5,4,3,2,1,0:T(8,128)(2,1)} custom-call(bf16[64,200,128]{2,1,0:T(8,128)(2,1)S(1)} %all_to_all.10.received_ref), custom_call_target="tpu_custom_call" | custom-call | tf_op jit(solution)/shard_map/product/pallas_call | solution.py:397
  62.3 5.5 %all-to-all-start.1 = ((bf16[128,7,8,128]{3,2,1,0:T(8,128)(2,1)}), bf16[128,7,8,128]{3,2,1,0:T(8,128)(2,1)}, u32[]{:S(2)}, u32[]{:S(2)}) async-start(bf16[128,7,8,128]{3,2,1,0:T(8,128)(2,1)} %bitcast.5), calls=%async_computation.1 | async-start | bytes 3670016 | tf_op jit(solution)/shard_map/all_to_all | solution.py:414
  67.7 0.0 copy-start
  67.8 0.0 copy-start.1
  67.8 6.0 %gate.1.gate_ref = f32[112,7,8,128]{3,2,1,0:T(8,128)S(1)} custom-call(bf16[112,112,128]{2,1,0:T(8,128)(2,1)} %pair_ref.1, f32[1,128]{1,0:T(1,128)} %bitcast.14, bf16[128,128]{1,0:T(8,128)(2,1)} %weight_ref.2), custom_call_target="tpu_custom_call" | custom-call | flops 205520896 | bytes 8028160 | tf_op jit(solution)/shard_map/gate/pallas_call | solution.py:375
  73.8 20.1 %all-to-all-done.1.hidden_hbm = bf16[128,7,8,128]{3,2,1,0:T(8,128)(2,1)} async-done(((bf16[128,7,8,128]{3,2,1,0:T(8,128)(2,1)}), bf16[128,7,8,128]{3,2,1,0:T(8,128)(2,1)}, u32[]{:S(2)}, u32[]{:S(2)}) %all-to-all-start.1) | async-done | bytes 1835040 | tf_op jit(solution)/shard_map/all_to_all | solution.py:414
  93.9 0.0 copy-done
  93.9 0.0 copy-done.1
  93.9 4.1 %finish.1 = bf16[112,7,8,128]{3,2,1,0:T(8,128)(2,1)} custom-call(bf16[128,7,8,128]{3,2,1,0:T(8,128)(2,1)} %all-to-all-done.1.hidden_hbm, f32[112,7,8,128]{3,2,1,0:T(8,128)S(1)} %gate.1.gate_ref, f32[1,128]{1,0:T(1,128)S(1)} %bitcast.8, bf16[128,128]{1,0:T(8,128)(2,1)S(1)} %copy-done), custom_call_target="tpu_custom_call" | custom-call | tf_op jit(solution)/shard_map/finish/pallas_call | solution.py:418
Async XLA Ops:
  62.3 31.6 %all-to-all-start.1 = ((bf16[128,7,8,128]{3,2,1,0:T(8,128)(2,1)}), bf16[128,7,8,128]{3,2,1,0:T(8,128)(2,1)}, u32[]{:S(2)}, u32[]{:S(2)}) async-start(bf16[128,7,8,128]{3,2,1,0:T(8,128)(2,1)} %bitcast.5), calls=%async_computation.1 | async-start | bytes 3670016 | tf_op jit(solution)/shard_map/all_to_all | solution.py:414
  67.7 26.1 %copy-start = (bf16[128,128]{1,0:T(8,128)(2,1)S(1)}, bf16[128,128]{1,0:T(8,128)(2,1)}, u32[]{:S(2)}) copy-start(bf16[128,128]{1,0:T(8,128)(2,1)} %weight_ref.3) | copy-start | bytes 98308
  67.8 26.1 %copy-start.1 = (f32[128]{0:T(128)S(1)}, f32[128]{0:T(128)}, u32[]{:S(2)}) copy-start(f32[128]{0:T(128)} %param.18) | copy-start | bytes 1540

commit v8 on v7

--- a/solution.py
+++ b/solution.py
@@ -168,8 +168,7 @@
 
 
 def product_kernel(received_ref, out_hbm, right_a, right_b, right_c, right_d, out_scr, sems):
-    ch, rows, cols, groups = out_hbm.shape[:4]
-    tile = ch * groups * 8
+    rows, cols, tile = 8, 8, out_hbm.shape[1] // 8
     rights = (right_a, right_b, right_c, right_d)
     blocks_count, steps = len(rights), out_scr.shape[0]
     share, wide = cols // blocks_count, rows // steps
@@ -195,11 +194,12 @@
         at = (q % share) * tile
         rights[q // share][at : at + tile, :] = block.T[:tile]
 
-    def send(s, h, side):
+    def send(s, h):
+        width = share * tile
         return pltpu.make_async_copy(
-            out_scr.at[s, h, side],
-            out_hbm.at[side, pl.ds(wide * s, wide), pl.ds(share * h, share)],
-            sems.at[s, h, side],
+            out_scr.at[s, h],
+            out_hbm.at[pl.ds(wide * s, wide), pl.ds(h * width, width)],
+            sems.at[s, h],
         )
 
     def multiply(s, h):
@@ -211,13 +211,10 @@
         ]
         hidden = jnp.dot(
             rights[h][...], jnp.concatenate(lefts, axis=1), preferred_element_type=f32
-        )
+        ).astype(bf16)
         for p in range(wide):
-            own = hidden[:, p * lanes : (p + 1) * lanes].reshape(share, ch, groups, 8, lanes)
-            for side in range(ch):
-                out_scr[s, h, side, p] = own[:, side].astype(bf16)
-        for side in range(ch):
-            send(s, h, side).start()
+            out_scr[s, h, p] = hidden[:, p * lanes : (p + 1) * lanes]
+        send(s, h).start()
 
     for q in range(share):
         turn(q)
@@ -228,8 +225,7 @@
             multiply(s, h)
     for h in range(blocks_count):
         for s in range(steps):
-            for side in range(ch):
-                send(s, h, side).wait()
+            send(s, h).wait()
 
 
 def finish_kernel(
@@ -257,13 +253,17 @@
     def fetch_hidden(g):
         return pltpu.make_async_copy(hidden_hbm.at[:, g], hidden_scr.at[g], hidden_sems.at[g])
 
-    def send(g):
-        return pltpu.make_async_copy(out_scr.at[g], out_hbm.at[:, g], out_sems.at[g])
+    def send(g, n):
+        own = pl.ds(n * (tile // 2), tile // 2)
+        return pltpu.make_async_copy(out_scr.at[g, own], out_hbm.at[own, g], out_sems.at[g, n])
 
     for g in range(groups):
         fetch_hidden(g).start()
     scaled = jnp.broadcast_to(gain_ref[...], (channels, channels)).T * weight_ref[...].astype(f32)
-    weight_scr[...] = scaled.astype(bf16)
+    part = channels // 2
+    for side in range(2):
+        turn_a[pl.ds(side, part, stride=2), :] = scaled[side * part : (side + 1) * part]
+    weight_scr[...] = turn_a[:channels, :].astype(bf16)
 
     def tree(terms):
         while len(terms) > 1:
@@ -310,12 +310,13 @@
         for j in range(8):
             if 2 <= s:
                 multiply(s - 2, j)
+                if j % 4 == 3:
+                    send(s - 2, j // 4).start()
             if 1 <= s < groups + 1:
                 project(s - 1, j)
-        if 2 <= s:
-            send(s - 2).start()
     for g in range(groups):
-        send(g).wait()
+        for n in range(2):
+            send(g, n).wait()
 
 
 def shards(
@@ -398,22 +399,23 @@
         product_kernel,
         in_specs=[vmem],
         out_specs=anywhere,
-        out_shape=jax.ShapeDtypeStruct((ch, rows, cols, groups, 8, lanes), bf16),
+        out_shape=jax.ShapeDtypeStruct((rows, cols * tile, lanes), bf16),
         scratch_shapes=[
             right_shape,
             right_shape,
             right_shape,
             right_shape,
-            pltpu.VMEM((2, 4, ch, rows // 2, cols // 4, groups, 8, lanes), bf16),
-            pltpu.SemaphoreType.DMA((2, 4, ch)),
+            pltpu.VMEM((2, 4, rows // 2, cols * tile // 4, lanes), bf16),
+            pltpu.SemaphoreType.DMA((2, 4)),
         ],
         compiler_params=limit,
         name="product",
     )(received)
 
     parts = lax.all_to_all(
-        hidden.reshape(channels, groups, 8, lanes), ("ch", "row", "col"), 0, 0, tiled=True
+        hidden.reshape(rows * cols * ch, half, lanes), ("row", "col", "ch"), 0, 0, tiled=True
     )
+    parts = parts.reshape(channels, groups, 8, lanes)
 
     update = pl.pallas_call(
         finish_kernel,
@@ -431,7 +433,7 @@
             pltpu.VMEM((2, 8, lanes), f32),
             pltpu.VMEM((2, 8, lanes), f32),
             pltpu.SemaphoreType.DMA((groups,)),
-            pltpu.SemaphoreType.DMA((groups,)),
+            pltpu.SemaphoreType.DMA((groups, 2)),
         ],
         compiler_params=limit,
         name="finish",

time: 98.7 us -> 99.7 us (1.010)
  waiting for transfers between devices: 20.1 us -> 21.6 us
    all_to_all x1, waiting for transfers between devices: 20.1 us -> 21.6 us  [shards(): lax.all_to_all(hidden.reshape(rows * cols * ch, half, lanes), ('row', 'co...]
where the time goes in v8:
time: 99.7 us; the launch traced here: 99.4 us
  blocking collectives  52.8 us (53%)
  waiting for transfers between devices  21.6 us (22%)
  Pallas kernels  19.5 us (20%)
  starting transfers between devices  5.46 us (5%)
    all_to_all x1, blocking collectives, shards(): received = lax.all_to_all(message, ('row', 'col'), 0, 0, tiled=True)  52.8 us
    all_to_all x1, waiting for transfers between devices, shards(): lax.all_to_all(hidden.reshape(rows * cols * ch, half, lanes), ('row', 'co...  21.6 us
    pallas_call x1, Pallas kernels, shards(): pl.pallas_call(project_kernel, in_specs=[anywhere] * 7, out_specs=vmem, o...  5.99 us
    pallas_call x1, Pallas kernels, shards(): pl.pallas_call(gate_kernel, grid=(tile // chunk,), in_specs=[pl.BlockSpec...  5.98 us
    all_to_all x1, starting transfers between devices, shards(): lax.all_to_all(hidden.reshape(rows * cols * ch, half, lanes), ('row', 'co...  5.46 us
    pallas_call x1, Pallas kernels, shards(): pl.pallas_call(finish_kernel, in_specs=[anywhere, vmem, vmem, vmem], out_...  4.14 us
    pallas_call x1, Pallas kernels, shards(): pl.pallas_call(product_kernel, in_specs=[vmem], out_specs=anywhere, out_s...  3.36 us
  transfers between devices with their start and end apart: 1, of which 1 were waited for; matrix products, arithmetic and copies ran while one was open for 0% of the time, Pallas kernels for 6%

profile of v8, /device:TPU:1, one launch (start us, length us, event | category | flops | bytes accessed | tf_op | source)
XLA Modules:
  0.0 99.4 jit_solution(12717223669172626098)
XLA Ops:
  0.0 6.0 %project.1 = bf16[64,200,128]{2,1,0:T(8,128)(2,1)S(1)} custom-call(bf16[112,112,128]{2,1,0:T(8,128)(2,1)} %pair_ref.1, s32[112,112]{1,0:T(8,128)} %mask_hbm.1, f32[1,128]{1,0:T(1,128)} %bitcast.14, bf16[64,128]{1,0:T(8,128)(2,1)} %bitcast.10, bf16[64,128]{1,0:T(8,128)(2,1)} %bitcast.11, bf16[64,128]{1,0:T(8,128)(2,1)} %bitcast.12, bf16[64,128]{1,0:T(8,128)(2,1)} %bitcast.13), custom_call_target="tpu_custom_call" | custom-call | tf_op jit(solution)/shard_map/project/pallas_call | solution.py:349
  6.0 52.8 %all_to_all.10.received_ref = bf16[64,200,128]{2,1,0:T(8,128)(2,1)S(1)} all-to-all(bf16[64,200,128]{2,1,0:T(8,128)(2,1)S(1)} %project.1), channel_id=1, replica_groups=mesh['row'=8,'col'=8,'ch'=2] {'row','col'}, dimensions={0} | all-to-all | bytes 6553600 | tf_op jit(solution)/shard_map/all_to_all | solution.py:395
  58.8 3.4 %product.1 = bf16[8,896,128]{2,1,0:T(8,128)(2,1)} custom-call(bf16[64,200,128]{2,1,0:T(8,128)(2,1)S(1)} %all_to_all.10.received_ref), custom_call_target="tpu_custom_call" | custom-call | tf_op jit(solution)/shard_map/product/pallas_call | solution.py:398
  62.2 5.5 %all-to-all-start.1 = ((bf16[128,56,128]{2,1,0:T(8,128)(2,1)}), bf16[128,56,128]{2,1,0:T(8,128)(2,1)}, u32[]{:S(2)}, u32[]{:S(2)}) async-start(bf16[128,56,128]{2,1,0:T(8,128)(2,1)} %bitcast.5), calls=%async_computation.1 | async-start | bytes 3670016 | tf_op jit(solution)/shard_map/all_to_all | solution.py:415
  67.6 0.0 copy-start
  67.6 0.0 copy-start.1
  67.7 6.0 %gate.1.gate_ref = f32[112,7,8,128]{3,2,1,0:T(8,128)S(1)} custom-call(bf16[112,112,128]{2,1,0:T(8,128)(2,1)} %pair_ref.1, f32[1,128]{1,0:T(1,128)} %bitcast.15, bf16[128,128]{1,0:T(8,128)(2,1)} %weight_ref.2), custom_call_target="tpu_custom_call" | custom-call | flops 205520896 | bytes 8028160 | tf_op jit(solution)/shard_map/gate/pallas_call | solution.py:376
  73.7 21.6 %all-to-all-done.1 = bf16[128,56,128]{2,1,0:T(8,128)(2,1)} async-done(((bf16[128,56,128]{2,1,0:T(8,128)(2,1)}), bf16[128,56,128]{2,1,0:T(8,128)(2,1)}, u32[]{:S(2)}, u32[]{:S(2)}) %all-to-all-start.1) | async-done | bytes 1835040 | tf_op jit(solution)/shard_map/all_to_all | solution.py:415
  95.2 0.0 copy-done
  95.2 0.0 copy-done.1
  95.2 4.1 %finish.1 = bf16[112,7,8,128]{3,2,1,0:T(8,128)(2,1)} custom-call(bf16[128,7,8,128]{3,2,1,0:T(8,128)(2,1)} %bitcast.6.hidden_hbm, f32[112,7,8,128]{3,2,1,0:T(8,128)S(1)} %gate.1.gate_ref, f32[1,128]{1,0:T(1,128)S(1)} %bitcast.9, bf16[128,128]{1,0:T(8,128)(2,1)S(1)} %copy-done), custom_call_target="tpu_custom_call" | custom-call | tf_op jit(solution)/shard_map/finish/pallas_call | solution.py:420
Async XLA Ops:
  62.2 33.0 %all-to-all-start.1 = ((bf16[128,56,128]{2,1,0:T(8,128)(2,1)}), bf16[128,56,128]{2,1,0:T(8,128)(2,1)}, u32[]{:S(2)}, u32[]{:S(2)}) async-start(bf16[128,56,128]{2,1,0:T(8,128)(2,1)} %bitcast.5), calls=%async_computation.1 | async-start | bytes 3670016 | tf_op jit(solution)/shard_map/all_to_all | solution.py:415
  67.6 27.6 %copy-start = (bf16[128,128]{1,0:T(8,128)(2,1)S(1)}, bf16[128,128]{1,0:T(8,128)(2,1)}, u32[]{:S(2)}) copy-start(bf16[128,128]{1,0:T(8,128)(2,1)} %weight_ref.3) | copy-start | bytes 98308
  67.6 27.6 %copy-start.1 = (f32[128]{0:T(128)S(1)}, f32[128]{0:T(128)}, u32[]{:S(2)}) copy-start(f32[128]{0:T(128)} %param.18) | copy-start | bytes 1540

commit v9 on v7

--- a/solution.py
+++ b/solution.py
@@ -178,8 +178,8 @@
     def turn(q):
         blocks = []
         for r in range(rows):
-            upper = received_ref[r * cols + q, :tile].astype(f32)
-            lower = received_ref[r * cols + q, tile:].astype(f32)
+            upper = received_ref[q * rows + r, :tile].astype(f32)
+            lower = received_ref[q * rows + r, tile:].astype(f32)
             parts = [jnp.where(lane < edge, lower, upper[: tile - spill])]
             for p in range(3):
                 pieces = [
@@ -205,7 +205,7 @@
     def multiply(s, h):
         lefts = [
             jnp.concatenate(
-                [received_ref[r * cols + wide * s + p, :tile] for r in range(rows)], axis=0
+                [received_ref[(wide * s + p) * rows + r, :tile] for r in range(rows)], axis=0
             )
             for p in range(wide)
         ]
@@ -263,7 +263,11 @@
     for g in range(groups):
         fetch_hidden(g).start()
     scaled = jnp.broadcast_to(gain_ref[...], (channels, channels)).T * weight_ref[...].astype(f32)
-    weight_scr[...] = scaled.astype(bf16)
+    turn_a[:channels, :] = scaled
+    for at in range(0, channels, 8):
+        first = at // 64 * 64 + at % 64 // 8
+        turn_b[at : at + 8, :] = turn_a[pl.ds(first, 8, stride=8), :]
+    weight_scr[...] = turn_b[:channels, :].astype(bf16)
 
     def tree(terms):
         while len(terms) > 1:
@@ -391,7 +395,7 @@
         name="gate",
     )(pair, gain_row, stay(w_gate))
 
-    received = lax.all_to_all(message, ("row", "col"), 0, 0, tiled=True)
+    received = lax.all_to_all(message, ("col", "row"), 0, 0, tiled=True)
 
     right_shape = pltpu.VMEM((cols * tile // 4, rows * tile), bf16)
     hidden = pl.pallas_call(

time: 98.7 us -> 99.2 us (level)
  no operation moved by 1% of the time
where the time goes in v9:
time: 99.2 us; the launch traced here: 98.5 us
  blocking collectives  52.5 us (53%)
  waiting for transfers between devices  20.1 us (20%)
  Pallas kernels  19.5 us (20%)
  starting transfers between devices  6.27 us (6%)
    all_to_all x1, blocking collectives, shards(): received = lax.all_to_all(message, ('col', 'row'), 0, 0, tiled=True)  52.5 us
    all_to_all x1, waiting for transfers between devices, shards(): lax.all_to_all(hidden.reshape(channels, groups, 8, lanes), ('ch', 'row',...  20.1 us
    all_to_all x1, starting transfers between devices, shards(): lax.all_to_all(hidden.reshape(channels, groups, 8, lanes), ('ch', 'row',...  6.27 us
    pallas_call x1, Pallas kernels, shards(): pl.pallas_call(project_kernel, in_specs=[anywhere] * 7, out_specs=vmem, o...  5.99 us
    pallas_call x1, Pallas kernels, shards(): pl.pallas_call(gate_kernel, grid=(tile // chunk,), in_specs=[pl.BlockSpec...  5.98 us
    pallas_call x1, Pallas kernels, shards(): pl.pallas_call(finish_kernel, in_specs=[anywhere, vmem, vmem, vmem], out_...  4.1 us
    pallas_call x1, Pallas kernels, shards(): pl.pallas_call(product_kernel, in_specs=[vmem], out_specs=anywhere, out_s...  3.47 us
  transfers between devices with their start and end apart: 1, of which 1 were waited for; matrix products, arithmetic and copies ran while one was open for 0% of the time, Pallas kernels for 6%

profile of v9, /device:TPU:1, one launch (start us, length us, event | category | flops | bytes accessed | tf_op | source)
XLA Modules:
  0.0 98.5 jit_solution(9678841566446074991)
XLA Ops:
  0.0 6.0 %project.1 = bf16[64,200,128]{2,1,0:T(8,128)(2,1)S(1)} custom-call(bf16[112,112,128]{2,1,0:T(8,128)(2,1)} %pair_ref.1, s32[112,112]{1,0:T(8,128)} %mask_hbm.1, f32[1,128]{1,0:T(1,128)} %bitcast.13, bf16[64,128]{1,0:T(8,128)(2,1)} %bitcast.9, bf16[64,128]{1,0:T(8,128)(2,1)} %bitcast.10, bf16[64,128]{1,0:T(8,128)(2,1)} %bitcast.11, bf16[64,128]{1,0:T(8,128)(2,1)} %bitcast.12), custom_call_target="tpu_custom_call" | custom-call | tf_op jit(solution)/shard_map/project/pallas_call | solution.py:352
  6.0 52.5 %all_to_all.10.received_ref = bf16[64,200,128]{2,1,0:T(8,128)(2,1)S(1)} all-to-all(bf16[64,200,128]{2,1,0:T(8,128)(2,1)S(1)} %project.1), channel_id=1, replica_groups=mesh['row'=8,'col'=8,'ch'=2] {'col','row'}, dimensions={0} | all-to-all | bytes 6553600 | tf_op jit(solution)/shard_map/all_to_all | solution.py:398
  58.5 3.5 %product.1 = bf16[2,8,8,7,8,128]{5,4,3,2,1,0:T(8,128)(2,1)} custom-call(bf16[64,200,128]{2,1,0:T(8,128)(2,1)S(1)} %all_to_all.10.received_ref), custom_call_target="tpu_custom_call" | custom-call | tf_op jit(solution)/shard_map/product/pallas_call | solution.py:401
  62.0 6.3 %all-to-all-start.1 = ((bf16[128,7,8,128]{3,2,1,0:T(8,128)(2,1)}), bf16[128,7,8,128]{3,2,1,0:T(8,128)(2,1)}, u32[]{:S(2)}, u32[]{:S(2)}) async-start(bf16[128,7,8,128]{3,2,1,0:T(8,128)(2,1)} %bitcast.5), calls=%async_computation.1 | async-start | bytes 3670016 | tf_op jit(solution)/shard_map/all_to_all | solution.py:418
  68.3 0.0 copy-start
  68.3 0.0 copy-start.1
  68.3 6.0 %gate.1.gate_ref = f32[112,7,8,128]{3,2,1,0:T(8,128)S(1)} custom-call(bf16[112,112,128]{2,1,0:T(8,128)(2,1)} %pair_ref.1, f32[1,128]{1,0:T(1,128)} %bitcast.14, bf16[128,128]{1,0:T(8,128)(2,1)} %weight_ref.2), custom_call_target="tpu_custom_call" | custom-call | flops 205520896 | bytes 8028160 | tf_op jit(solution)/shard_map/gate/pallas_call | solution.py:379
  74.3 20.1 %all-to-all-done.1.hidden_hbm = bf16[128,7,8,128]{3,2,1,0:T(8,128)(2,1)} async-done(((bf16[128,7,8,128]{3,2,1,0:T(8,128)(2,1)}), bf16[128,7,8,128]{3,2,1,0:T(8,128)(2,1)}, u32[]{:S(2)}, u32[]{:S(2)}) %all-to-all-start.1) | async-done | bytes 1835040 | tf_op jit(solution)/shard_map/all_to_all | solution.py:418
  94.4 0.0 copy-done
  94.4 0.0 copy-done.1
  94.4 4.1 %finish.1 = bf16[112,7,8,128]{3,2,1,0:T(8,128)(2,1)} custom-call(bf16[128,7,8,128]{3,2,1,0:T(8,128)(2,1)} %all-to-all-done.1.hidden_hbm, f32[112,7,8,128]{3,2,1,0:T(8,128)S(1)} %gate.1.gate_ref, f32[1,128]{1,0:T(1,128)S(1)} %bitcast.8, bf16[128,128]{1,0:T(8,128)(2,1)S(1)} %copy-done), custom_call_target="tpu_custom_call" | custom-call | tf_op jit(solution)/shard_map/finish/pallas_call | solution.py:422
Async XLA Ops:
  62.0 32.4 %all-to-all-start.1 = ((bf16[128,7,8,128]{3,2,1,0:T(8,128)(2,1)}), bf16[128,7,8,128]{3,2,1,0:T(8,128)(2,1)}, u32[]{:S(2)}, u32[]{:S(2)}) async-start(bf16[128,7,8,128]{3,2,1,0:T(8,128)(2,1)} %bitcast.5), calls=%async_computation.1 | async-start | bytes 3670016 | tf_op jit(solution)/shard_map/all_to_all | solution.py:418
  68.3 26.1 %copy-start = (bf16[128,128]{1,0:T(8,128)(2,1)S(1)}, bf16[128,128]{1,0:T(8,128)(2,1)}, u32[]{:S(2)}) copy-start(bf16[128,128]{1,0:T(8,128)(2,1)} %weight_ref.3) | copy-start | bytes 98308
  68.3 26.1 %copy-start.1 = (f32[128]{0:T(128)S(1)}, f32[128]{0:T(128)}, u32[]{:S(2)}) copy-start(f32[128]{0:T(128)} %param.18) | copy-start | bytes 1540

commit v10 on v7

--- a/solution.py
+++ b/solution.py
@@ -257,8 +257,9 @@
     def fetch_hidden(g):
         return pltpu.make_async_copy(hidden_hbm.at[:, g], hidden_scr.at[g], hidden_sems.at[g])
 
-    def send(g):
-        return pltpu.make_async_copy(out_scr.at[g], out_hbm.at[:, g], out_sems.at[g])
+    def send(g, n):
+        own = pl.ds(n * (tile // 2), tile // 2)
+        return pltpu.make_async_copy(out_scr.at[g, own], out_hbm.at[own, g], out_sems.at[g, n])
 
     for g in range(groups):
         fetch_hidden(g).start()
@@ -310,12 +311,13 @@
         for j in range(8):
             if 2 <= s:
                 multiply(s - 2, j)
+                if j % 4 == 3:
+                    send(s - 2, j // 4).start()
             if 1 <= s < groups + 1:
                 project(s - 1, j)
-        if 2 <= s:
-            send(s - 2).start()
     for g in range(groups):
-        send(g).wait()
+        for n in range(2):
+            send(g, n).wait()
 
 
 def shards(
@@ -431,7 +433,7 @@
             pltpu.VMEM((2, 8, lanes), f32),
             pltpu.VMEM((2, 8, lanes), f32),
             pltpu.SemaphoreType.DMA((groups,)),
-            pltpu.SemaphoreType.DMA((groups,)),
+            pltpu.SemaphoreType.DMA((groups, 2)),
         ],
         compiler_params=limit,
         name="finish",

time: 98.7 us -> 98.8 us (level)
  no operation moved by 1% of the time
where the time goes in v10:
time: 98.8 us; the launch traced here: 98 us
  blocking collectives  52.8 us (53%)
  waiting for transfers between devices  20.1 us (20%)
  Pallas kernels  19.6 us (20%)
  starting transfers between devices  5.46 us (6%)
    all_to_all x1, blocking collectives, shards(): received = lax.all_to_all(message, ('row', 'col'), 0, 0, tiled=True)  52.8 us
    all_to_all x1, waiting for transfers between devices, shards(): lax.all_to_all(hidden.reshape(channels, groups, 8, lanes), ('ch', 'row',...  20.1 us
    pallas_call x1, Pallas kernels, shards(): pl.pallas_call(project_kernel, in_specs=[anywhere] * 7, out_specs=vmem, o...  5.99 us
    pallas_call x1, Pallas kernels, shards(): pl.pallas_call(gate_kernel, grid=(tile // chunk,), in_specs=[pl.BlockSpec...  5.98 us
    all_to_all x1, starting transfers between devices, shards(): lax.all_to_all(hidden.reshape(channels, groups, 8, lanes), ('ch', 'row',...  5.46 us
    pallas_call x1, Pallas kernels, shards(): pl.pallas_call(finish_kernel, in_specs=[anywhere, vmem, vmem, vmem], out_...  4.15 us
    pallas_call x1, Pallas kernels, shards(): pl.pallas_call(product_kernel, in_specs=[vmem], out_specs=anywhere, out_s...  3.46 us
  transfers between devices with their start and end apart: 1, of which 1 were waited for; matrix products, arithmetic and copies ran while one was open for 0% of the time, Pallas kernels for 6%

profile of v10, /device:TPU:1, one launch (start us, length us, event | category | flops | bytes accessed | tf_op | source)
XLA Modules:
  0.0 98.0 jit_solution(6776846287062904262)
XLA Ops:
  0.0 6.0 %project.1 = bf16[64,200,128]{2,1,0:T(8,128)(2,1)S(1)} custom-call(bf16[112,112,128]{2,1,0:T(8,128)(2,1)} %pair_ref.1, s32[112,112]{1,0:T(8,128)} %mask_hbm.1, f32[1,128]{1,0:T(1,128)} %bitcast.13, bf16[64,128]{1,0:T(8,128)(2,1)} %bitcast.9, bf16[64,128]{1,0:T(8,128)(2,1)} %bitcast.10, bf16[64,128]{1,0:T(8,128)(2,1)} %bitcast.11, bf16[64,128]{1,0:T(8,128)(2,1)} %bitcast.12), custom_call_target="tpu_custom_call" | custom-call | tf_op jit(solution)/shard_map/project/pallas_call | solution.py:350
  6.0 52.8 %all_to_all.10.received_ref = bf16[64,200,128]{2,1,0:T(8,128)(2,1)S(1)} all-to-all(bf16[64,200,128]{2,1,0:T(8,128)(2,1)S(1)} %project.1), channel_id=1, replica_groups=mesh['row'=8,'col'=8,'ch'=2] {'row','col'}, dimensions={0} | all-to-all | bytes 6553600 | tf_op jit(solution)/shard_map/all_to_all | solution.py:396
  58.8 3.5 %product.1 = bf16[2,8,8,7,8,128]{5,4,3,2,1,0:T(8,128)(2,1)} custom-call(bf16[64,200,128]{2,1,0:T(8,128)(2,1)S(1)} %all_to_all.10.received_ref), custom_call_target="tpu_custom_call" | custom-call | tf_op jit(solution)/shard_map/product/pallas_call | solution.py:399
  62.3 5.5 %all-to-all-start.1 = ((bf16[128,7,8,128]{3,2,1,0:T(8,128)(2,1)}), bf16[128,7,8,128]{3,2,1,0:T(8,128)(2,1)}, u32[]{:S(2)}, u32[]{:S(2)}) async-start(bf16[128,7,8,128]{3,2,1,0:T(8,128)(2,1)} %bitcast.5), calls=%async_computation.1 | async-start | bytes 3670016 | tf_op jit(solution)/shard_map/all_to_all | solution.py:416
  67.7 0.0 copy-start
  67.8 0.0 copy-start.1
  67.8 6.0 %gate.1.gate_ref = f32[112,7,8,128]{3,2,1,0:T(8,128)S(1)} custom-call(bf16[112,112,128]{2,1,0:T(8,128)(2,1)} %pair_ref.1, f32[1,128]{1,0:T(1,128)} %bitcast.14, bf16[128,128]{1,0:T(8,128)(2,1)} %weight_ref.2), custom_call_target="tpu_custom_call" | custom-call | flops 205520896 | bytes 8028160 | tf_op jit(solution)/shard_map/gate/pallas_call | solution.py:377
  73.8 20.1 %all-to-all-done.1.hidden_hbm = bf16[128,7,8,128]{3,2,1,0:T(8,128)(2,1)} async-done(((bf16[128,7,8,128]{3,2,1,0:T(8,128)(2,1)}), bf16[128,7,8,128]{3,2,1,0:T(8,128)(2,1)}, u32[]{:S(2)}, u32[]{:S(2)}) %all-to-all-start.1) | async-done | bytes 1835040 | tf_op jit(solution)/shard_map/all_to_all | solution.py:416
  93.9 0.0 copy-done
  93.9 0.0 copy-done.1
  93.9 4.1 %finish.1 = bf16[112,7,8,128]{3,2,1,0:T(8,128)(2,1)} custom-call(bf16[128,7,8,128]{3,2,1,0:T(8,128)(2,1)} %all-to-all-done.1.hidden_hbm, f32[112,7,8,128]{3,2,1,0:T(8,128)S(1)} %gate.1.gate_ref, f32[1,128]{1,0:T(1,128)S(1)} %bitcast.8, bf16[128,128]{1,0:T(8,128)(2,1)S(1)} %copy-done), custom_call_target="tpu_custom_call" | custom-call | tf_op jit(solution)/shard_map/finish/pallas_call | solution.py:420
Async XLA Ops:
  62.3 31.6 %all-to-all-start.1 = ((bf16[128,7,8,128]{3,2,1,0:T(8,128)(2,1)}), bf16[128,7,8,128]{3,2,1,0:T(8,128)(2,1)}, u32[]{:S(2)}, u32[]{:S(2)}) async-start(bf16[128,7,8,128]{3,2,1,0:T(8,128)(2,1)} %bitcast.5), calls=%async_computation.1 | async-start | bytes 3670016 | tf_op jit(solution)/shard_map/all_to_all | solution.py:416
  67.7 26.1 %copy-start = (bf16[128,128]{1,0:T(8,128)(2,1)S(1)}, bf16[128,128]{1,0:T(8,128)(2,1)}, u32[]{:S(2)}) copy-start(bf16[128,128]{1,0:T(8,128)(2,1)} %weight_ref.3) | copy-start | bytes 98308
  67.8 26.1 %copy-start.1 = (f32[128]{0:T(128)S(1)}, f32[128]{0:T(128)}, u32[]{:S(2)}) copy-start(f32[128]{0:T(128)} %param.18) | copy-start | bytes 1540
